TPU v7x, 512 devices: a whole 4x8x8 slice. The times are simulated.
512 devices in a mesh: ctx: 32 (over y, z_hi), tp: 8 (over x, z_lo), grp: 2 (over core).
Axes of the slice: x: 4, y: 8, z: 8 (z_hi: 4, z_lo: 2; z = z_hi * 2 + z_lo), core: 2. Of those that a mesh axis runs over, the one named last changes fastest.
Arguments:
- queries: bfloat16 [2, 4096, 8192], P('grp', 'ctx', 'tp')
- rotated_new_keys: bfloat16 [2, 4096, 1024], P('grp', 'ctx', 'tp')
- fresh_token_values: bfloat16 [2, 4096, 1024], P('grp', 'ctx', 'tp'), may hold values from -6 to 6
- prefix_cached_keys: bfloat16 [2, 2048, 1024], P('grp', 'ctx', 'tp'), may hold values from -6 to 6
- prefix_cached_values: bfloat16 [2, 2048, 1024], P('grp', 'ctx', 'tp'), may hold values from -6 to 6
- prompt_len: int32 [2], P('grp'), may hold values from 1024 to 4096, as said below
- prefix_len: int32 [2], P('grp'), may hold values from 0 to 2048, as said below
- decode_page_slots: int32 [2, 256], P('grp'), may hold values from 0 to 255, each once within a row
Outputs:
- attended: bfloat16 [2, 4096, 8192], P('grp', 'ctx', 'tp')
- key_pool: bfloat16 [2, 4096, 1024], P('grp', ('ctx', 'tp'))
- value_pool: bfloat16 [2, 4096, 1024], P('grp', ('ctx', 'tp'))
Inputs may be any that keep to these rules, and one draw needn't show every extreme that they name: `prompt_len`: one of the two groups has a full prompt. `prefix_len`: one of the two groups has a full cached prefix.
All inputs are finite; a program needn't handle non-finite values.
Results may differ from a plain program's by a relative error of at most 0.01.
Values may be sent and summed in bfloat16 or wider, within the bound.
No kernel may reach another device: no remote copies, remote signals or barrier semaphores. Data moves between devices by JAX's collectives and lax.ppermute only.
A program may use at most 64 MiB of HBM per device.

v0:
```python
import jax
import jax.numpy as jnp
from jax import lax
from jax.sharding import PartitionSpec as P

HEAD_SIZE = 128
PAGE_TOKENS = 16


def partner(value, axis, apart):
    return lax.ppermute(value, axis, [(i, i ^ 1 << apart) for i in range(lax.axis_size(axis))])


def softmax_update(state, query_heads, kpiece, vpiece, visible):
    top, total, summed = state
    count = kpiece.shape[0]
    kv_heads = query_heads.shape[1]
    keys = kpiece.reshape(count, kv_heads, HEAD_SIZE)
    vals = vpiece.reshape(count, kv_heads, HEAD_SIZE)
    scores = jnp.einsum(
        "qkgd,nkd->kgqn", query_heads, keys, preferred_element_type=jnp.float32
    ) * HEAD_SIZE ** (-0.5)
    scores = jnp.where(visible[None, None], scores, jnp.float32(-1e30))
    new_top = jnp.maximum(top, jnp.max(scores, axis=-1))
    factor = jnp.exp(top - new_top)
    weights = jnp.where(visible[None, None], jnp.exp(scores - new_top[..., None]), jnp.float32(0.0))
    total = total * factor + jnp.sum(weights, axis=-1)
    probs = weights.astype(jnp.bfloat16)
    summed = summed * factor[..., None] + jnp.einsum(
        "kgqn,nkd->kgqd", probs, vals, preferred_element_type=jnp.float32
    )
    return (new_top, total, summed)


def pick_rows(wanted, usable, piece):
    count = piece.shape[0]
    onehot = (wanted[:, None] == jnp.arange(count, dtype=jnp.int32)[None, :]) & usable[:, None]
    return jnp.dot(onehot.astype(jnp.bfloat16), piece, preferred_element_type=jnp.float32)


def body(
    queries,
    rotated_new_keys,
    fresh_token_values,
    prefix_cached_keys,
    prefix_cached_values,
    prompt_len,
    prefix_len,
    decode_page_slots,
):
    n_ctx = lax.axis_size("ctx")
    n_tp = lax.axis_size("tp")
    ctx_index = lax.axis_index("ctx")
    rows = queries.shape[1]
    kv_heads = rotated_new_keys.shape[2] // HEAD_SIZE
    query_per_key_ratio = queries.shape[2] // HEAD_SIZE // kv_heads
    length = prompt_len[0]
    prefix = prefix_len[0]
    local_q = queries[0]
    qpos = ctx_index * rows + jnp.arange(rows, dtype=jnp.int32)
    query_heads = local_q.reshape(rows, kv_heads, query_per_key_ratio, HEAD_SIZE)
    start_state = (
        jnp.full((kv_heads, query_per_key_ratio, rows), -1e30, jnp.float32),
        jnp.zeros((kv_heads, query_per_key_ratio, rows), jnp.float32),
        jnp.zeros((kv_heads, query_per_key_ratio, rows, HEAD_SIZE), jnp.float32),
    )
    kpiece = lax.all_gather(prefix_cached_keys[0], "ctx", axis=0, tiled=True)
    vpiece = lax.all_gather(prefix_cached_values[0], "ctx", axis=0, tiled=True)
    slots = jnp.arange(kpiece.shape[0], dtype=jnp.int32)
    visible = jnp.broadcast_to((slots < prefix)[None, :], (rows, kpiece.shape[0]))
    state = lax.cond(
        jnp.int32(0) < prefix,
        lambda inner: softmax_update(inner, query_heads, kpiece, vpiece, visible),
        lambda inner: inner,
        start_state,
    )
    npages = decode_page_slots.shape[1]
    per_device = npages // (n_ctx * n_tp)
    slots_here = ctx_index * n_tp * per_device + jnp.arange(n_tp * per_device, dtype=jnp.int32)
    page_ids = jnp.arange(npages, dtype=jnp.int32)
    pages_here = jnp.sum(
        jnp.where(decode_page_slots[0][None, :] == slots_here[:, None], page_ids[None, :], 0),
        axis=1,
    )
    wanted = (
        pages_here[:, None] * PAGE_TOKENS + jnp.arange(PAGE_TOKENS, dtype=jnp.int32)[None, :]
    ).reshape(-1)
    usable = wanted < length
    width = rotated_new_keys.shape[2]
    last_query = jnp.max(qpos)
    fold_init = state
    pieces = (
        lax.all_gather(rotated_new_keys[0], "ctx", axis=0, tiled=True),
        lax.all_gather(fresh_token_values[0], "ctx", axis=0, tiled=True),
    )
    attend_kpiece = pieces[0]
    attend_vpiece = pieces[1]
    start = jnp.int32(0)
    positions = jnp.arange(attend_kpiece.shape[0], dtype=jnp.int32)
    attend_visible = (positions[None, :] < length) & (positions[None, :] <= qpos[:, None])
    folded = lax.cond(
        (start <= last_query) & (start < length),
        lambda inner: softmax_update(
            inner, query_heads, attend_kpiece, attend_vpiece, attend_visible
        ),
        lambda inner: inner,
        fold_init,
    )
    state = folded
    pieces = (
        lax.all_gather(rotated_new_keys[0], "ctx", axis=0, tiled=True),
        lax.all_gather(fresh_token_values[0], "ctx", axis=0, tiled=True),
    )
    kpages = pick_rows(wanted, usable, pieces[0])
    vpages = pick_rows(wanted, usable, pieces[1])
    top, total, summed = state
    result = summed / total[..., None]
    result = result.transpose(2, 0, 1, 3).reshape(rows, kv_heads * query_per_key_ratio * HEAD_SIZE)
    result = jnp.where((qpos < length)[:, None], result, jnp.float32(0.0)).astype(jnp.bfloat16)
    kpages = kpages.astype(jnp.bfloat16).reshape(n_tp, per_device * PAGE_TOKENS, width)
    vpages = vpages.astype(jnp.bfloat16).reshape(n_tp, per_device * PAGE_TOKENS, width)
    kpages, vpages = (
        lax.all_to_all(kpages, "tp", split_axis=0, concat_axis=2, tiled=True),
        lax.all_to_all(vpages, "tp", split_axis=0, concat_axis=2, tiled=True),
    )
    kpages, vpages = partner((kpages, vpages), "grp", 0)
    return (result[None], kpages, vpages)


def solution(mesh):
    in_specs = (
        P("grp", "ctx", "tp"),
        P("grp", "ctx", "tp"),
        P("grp", "ctx", "tp"),
        P("grp", "ctx", "tp"),
        P("grp", "ctx", "tp"),
        P("grp"),
        P("grp"),
        P("grp", None),
    )
    out_specs = (
        P("grp", "ctx", "tp"),
        P("grp", ("ctx", "tp"), None),
        P("grp", ("ctx", "tp"), None),
    )
    return jax.shard_map(body, mesh=mesh, in_specs=in_specs, out_specs=out_specs, check_vma=False)
```

profile of v0, /device:TPU:1, one launch (start us, length us, event | category | flops | bytes accessed | tf_op | source)
XLA Modules:
  0.0 243.5 jit_solution(17023169195273900949)
XLA Ops:
  7.2 0.7 all-gather.7.cloned.1.call-update
  7.9 0.7 all-gather.9.cloned.1.call-update
  11.2 1.1 copy.26
  12.4 0.9 select_reduce_fusion
  13.4 78.8 %all-gather = bf16[1,2048,128]{2,1,0:T(8,128)(2,1)S(1)} all-gather(bf16[1,64,128]{2,1,0:T(8,128)(2,1)} %param.15), channel_id=2, replica_groups=mesh['ctx'=32,'tp'=8,'grp'=2] {'ctx'}, dimensions={1}, use_global_device_ids=true | all-gather | bytes 540672 | tf_op jit(solution)/shard_map/all_gather | solution.py:67
  92.2 65.9 %all-gather.1 = bf16[1,2048,128]{2,1,0:T(8,128)(2,1)S(1)} all-gather(bf16[1,64,128]{2,1,0:T(8,128)(2,1)} %param.16), channel_id=3, replica_groups=mesh['ctx'=32,'tp'=8,'grp'=2] {'ctx'}, dimensions={1}, use_global_device_ids=true | all-gather | bytes 540672 | tf_op jit(solution)/shard_map/all_gather | solution.py:68
  158.1 7.8 %conditional.2 = (f32[1,8,128]{2,1,0:T(8,128)S(1)}, f32[1,8,128]{2,1,0:T(8,128)S(1)}, f32[1,8,128,128]{3,2,1,0:T(8,128)S(1)}) conditional(s32[]{:T(128)} %convert_element_type.31, () %tuple.23, (s32[]{:T(128)}, s32[1,2048]{1,0:T(1,128)S(1)}, bf16[128,1,8,128]{0,3,2,1:T(8,128)(2,1)S(1)}, bf16[2048,128]{1,0:T(8,128)(2,1)S(1)}, ...), branch_computations={%region_1.2_spmd, %region_2.5_spmd} | conditional | flops 1101143040 | bytes 27066396 | solution.py:71
  158.8 1.3 bitcast_reduce_fusion
  160.2 2.7 %fusion.3 = f32[8,128]{1,0:T(8,128)S(1)} fusion(f32[2048,128,8]{1,0,2:T(8,128)S(1)} %get-tuple-element.118, f32[8,128]{1,0:T(8,128)S(1)} %get-tuple-element.116, pred[2048]{0:T(1024)(128)(4,1)S(1)} %compare_reduce_fusion), kind=kLoop, calls=%fused_computation.6 | loop fusion | flops 10484736 | bytes 8398848 | tf_op jit(solution)/shard_map/cond/branch_1_fun/reduce_sum | solution.py:27
  162.9 3.0 %fusion.12 = f32[1,8,128,128]{3,2,1,0:T(8,128)S(1)} fusion(f32[2048,128,8]{1,0,2:T(8,128)S(1)} %get-tuple-element.118, f32[8,128]{1,0:T(8,128)S(1)} %get-tuple-element.116, pred[2048]{0:T(1024)(128)(4,1)S(1)} %compare_reduce_fusion, bf16[2048,128]{1,0:T(8,128)(2,1)S(1)} %get-tuple-element.52, f32[8,128]{1,0:T(8,128)S(1)} %get-tuple-element.115), kind=kOutput, calls=%fused_computation.12 | convolution fusion | flops 547487744 | bytes 9447424 | tf_op jit(solution)/shard_map/cond/branch_1_fun/kgqn,nkd->kgqd/dot_general | solution.py:29
  166.0 2.5 %fusion.50 = bf16[128,128]{1,0:T(8,128)(2,1)} fusion(s32[128]{0:T(128)S(1)} %add.81, pred[128]{0:T(512)(128)(4,1)S(1)} %broadcast_compare_fusion, bf16[1,4096,128]{2,1,0:T(8,128)(2,1)} %all-gather.7.cloned.1.call-done), kind=kOutput, calls=%fused_computation.54 | convolution fusion | flops 135282688 | bytes 1081984 | tf_op jit(solution)/shard_map/dot_general | solution.py:38
  168.4 4.4 %all-to-all-start = ((bf16[8,16,128]{2,1,0:T(8,128)(2,1)}), bf16[8,16,128]{2,1,0:T(8,128)(2,1)S(1)}, u32[]{:S(2)}, u32[]{:S(2)}) async-start(bf16[8,16,128]{2,1,0:T(8,128)(2,1)} %bitcast.31), calls=%async_computation | async-start | bytes 65536 | tf_op jit(solution)/shard_map/all_to_all | solution.py:123
  172.8 7.7 %all-gather.9.cloned.1.call-done = bf16[1,4096,128]{2,1,0:T(8,128)(2,1)} async-done(((bf16[1,128,128]{2,1,0:T(8,128)(2,1)}), bf16[1,4096,128]{2,1,0:T(8,128)(2,1)}) %all-gather.9.cloned.1.call-update) | async-done | bytes 1048592 | tf_op jit(solution)/shard_map/all_gather | solution.py:94
  180.7 15.7 %conditional.3 = ((f32[1,8,128]{2,1,0:T(8,128)S(1)}, f32[1,8,128,128]{3,2,1,0:T(8,128)S(1)})) conditional(s32[]{:T(128)} %convert_element_type.30, (f32[1,8,128]{2,1,0:T(8,128)S(1)}, f32[1,8,128,128]{3,2,1,0:T(8,128)S(1)}) %tuple.25, (s32[]{:T(128)}, s32[1,4096]{1,0:T(1,128)S(1)}, s32[]{:T(128)}, s32[128,1]{0,1:T(1,128)S(1)}, ...), branch_computations={%region_5.6_spmd, %region_6.0_spmd} | conditional | flops 2203328512 | bytes 62211644 | solution.py:101
  180.9 0.7 compare_reduce_fusion.1
  181.6 2.1 compare_and_fusion
  183.7 3.7 %fusion.23 = (f32[8,128]{1,0:T(8,128)S(1)}, f32[4096,128,8]{1,0,2:T(8,128)S(1)}) fusion(pred[128,4096]{0,1:T(8,128)(4,1)S(1)} %compare_and_fusion, bf16[128,1,8,128]{0,3,2,1:T(8,128)(2,1)S(1)} %get-tuple-element.103, bf16[4096,128]{1,0:T(8,128)(2,1)} %get-tuple-element.60), kind=kOutput, calls=%fused_computation.27 | convolution fusion | flops 1086323712 | bytes 18616320 | tf_op jit(solution)/shard_map/cond/branch_1_fun/qkgd,nkd->kgqn/dot_general | solution.py:20
  187.4 4.0 %fusion.25 = f32[8,128]{1,0:T(8,128)S(1)} fusion(f32[4096,128,8]{1,0,2:T(8,128)S(1)} %get-tuple-element.114, f32[8,128]{1,0:T(8,128)S(1)} %get-tuple-element.112, pred[128,4096]{0,1:T(8,128)(4,1)S(1)} %compare_and_fusion), kind=kLoop, calls=%fused_computation.29 | loop fusion | flops 20970496 | bytes 17309696 | tf_op jit(solution)/shard_map/cond/branch_1_fun/reduce_sum | solution.py:27
  191.5 4.8 %fusion.33 = f32[1,8,128,128]{3,2,1,0:T(8,128)S(1)} fusion(f32[4096,128,8]{1,0,2:T(8,128)S(1)} %get-tuple-element.114, f32[8,128]{1,0:T(8,128)S(1)} %get-tuple-element.112, pred[128,4096]{0,1:T(8,128)(4,1)S(1)} %compare_and_fusion, bf16[4096,128]{1,0:T(8,128)(2,1)S(1)} %copy-done, f32[1,8,128,128]{3,2,1,0:T(8,128)S(1)} %get-tuple-element.62, ...), kind=kOutput, calls=%fused_computation.35 | convolution fusion | flops 1094975488 | bytes 19406848 | tf_op jit(solution)/shard_map/cond/branch_1_fun/kgqn,nkd->kgqd/dot_general | solution.py:29
  196.3 2.5 %fusion.53 = bf16[128,128]{1,0:T(8,128)(2,1)} fusion(s32[128]{0:T(128)S(1)} %add.81, pred[128]{0:T(512)(128)(4,1)S(1)} %broadcast_compare_fusion, bf16[1,4096,128]{2,1,0:T(8,128)(2,1)} %all-gather.9.cloned.1.call-done), kind=kOutput, calls=%fused_computation.55 | convolution fusion | flops 135282688 | bytes 1081984 | tf_op jit(solution)/shard_map/dot_general | solution.py:38
  199.3 4.3 %all-to-all-start.1 = ((bf16[8,16,128]{2,1,0:T(8,128)(2,1)}), bf16[8,16,128]{2,1,0:T(8,128)(2,1)S(1)}, u32[]{:S(2)}, u32[]{:S(2)}) async-start(bf16[8,16,128]{2,1,0:T(8,128)(2,1)} %bitcast.34), calls=%async_computation.1 | async-start | bytes 65536 | tf_op jit(solution)/shard_map/all_to_all | solution.py:124
  203.6 24.8 %collective-permute-start = (bf16[1,16,1024]{2,1,0:T(8,128)(2,1)S(1)}, bf16[1,16,1024]{2,1,0:T(8,128)(2,1)S(1)}, u32[]{:S(2)}, u32[]{:S(2)}) collective-permute-start(bf16[1,16,1024]{2,1,0:T(8,128)(2,1)S(1)} %copy_bitcast_fusion.1), channel_id=1, source_target_pairs={{0,1},{1,0},{2,3},{3,2},{4,5},{5,4},{6,7},{7,6},{8,9},{9,8},{10,11... | collective-permute-start | bytes 98312 | tf_op jit(solution)/shard_map/ppermute | solution.py:11
  228.4 6.2 %collective-permute-start.1 = (bf16[1,16,1024]{2,1,0:T(8,128)(2,1)S(1)}, bf16[1,16,1024]{2,1,0:T(8,128)(2,1)S(1)}, u32[]{:S(2)}, u32[]{:S(2)}) collective-permute-start(bf16[1,16,1024]{2,1,0:T(8,128)(2,1)S(1)} %copy_bitcast_fusion), channel_id=1, source_target_pairs={{0,1},{1,0},{2,3},{3,2},{4,5},{5,4},{6,7},{7,6},{8,9},{9,8},{10,11... | collective-permute-start | bytes 98312 | tf_op jit(solution)/shard_map/ppermute | solution.py:11
  234.6 0.8 select_convert_fusion
  (33 shorter events, 3.6 us)
Async XLA Ops:
  7.2 158.8 %all-gather.7.cloned.1.call-start = ((), (), s32[]{:S(2)}) async-start(), calls=%async_computation.2 | async-start | bytes 1081344 | tf_op jit(solution)/shard_map/all_gather | solution.py:93
  7.9 172.6 %all-gather.9.cloned.1.call-start = ((), (), s32[]{:S(2)}) async-start(), calls=%async_computation.3 | async-start | bytes 1081344 | tf_op jit(solution)/shard_map/all_gather | solution.py:94
  168.4 30.9 %all-to-all-start = ((bf16[8,16,128]{2,1,0:T(8,128)(2,1)}), bf16[8,16,128]{2,1,0:T(8,128)(2,1)S(1)}, u32[]{:S(2)}, u32[]{:S(2)}) async-start(bf16[8,16,128]{2,1,0:T(8,128)(2,1)} %bitcast.31), calls=%async_computation | async-start | bytes 65536 | tf_op jit(solution)/shard_map/all_to_all | solution.py:123
  187.4 4.1 %copy-start = (bf16[4096,128]{1,0:T(8,128)(2,1)S(1)}, bf16[4096,128]{1,0:T(8,128)(2,1)}, u32[]{:S(2)}) copy-start(bf16[4096,128]{1,0:T(8,128)(2,1)} %get-tuple-element.63) | copy-start | bytes 3145732 | tf_op jit(solution)/shard_map/cond
  199.3 29.0 %all-to-all-start.1 = ((bf16[8,16,128]{2,1,0:T(8,128)(2,1)}), bf16[8,16,128]{2,1,0:T(8,128)(2,1)S(1)}, u32[]{:S(2)}, u32[]{:S(2)}) async-start(bf16[8,16,128]{2,1,0:T(8,128)(2,1)} %bitcast.34), calls=%async_computation.1 | async-start | bytes 65536 | tf_op jit(solution)/shard_map/all_to_all | solution.py:124
  203.6 31.8 %collective-permute-start = (bf16[1,16,1024]{2,1,0:T(8,128)(2,1)S(1)}, bf16[1,16,1024]{2,1,0:T(8,128)(2,1)S(1)}, u32[]{:S(2)}, u32[]{:S(2)}) collective-permute-start(bf16[1,16,1024]{2,1,0:T(8,128)(2,1)S(1)} %copy_bitcast_fusion.1), channel_id=1, source_target_pairs={{0,1},{1,0},{2,3},{3,2},{4,5},{5,4},{6,7},{7,6},{8,9},{9,8},{10,11... | collective-permute-start | bytes 98312 | tf_op jit(solution)/shard_map/ppermute | solution.py:11
  228.4 7.1 %collective-permute-start.1 = (bf16[1,16,1024]{2,1,0:T(8,128)(2,1)S(1)}, bf16[1,16,1024]{2,1,0:T(8,128)(2,1)S(1)}, u32[]{:S(2)}, u32[]{:S(2)}) collective-permute-start(bf16[1,16,1024]{2,1,0:T(8,128)(2,1)S(1)} %copy_bitcast_fusion), channel_id=1, source_target_pairs={{0,1},{1,0},{2,3},{3,2},{4,5},{5,4},{6,7},{7,6},{8,9},{9,8},{10,11... | collective-permute-start | bytes 98312 | tf_op jit(solution)/shard_map/ppermute | solution.py:11
Sparse Core Ops, SparseCore 0:
  11.2 86.3 all-gather.6
  100.7 79.7 all-gather.8
where the time goes:
time: 244 us
  blocking collectives  145 us (59%)
  starting transfers between devices  39.7 us (16%)
  matrix products  17.8 us (7%)
  between operations  16.1 us (7%)
  other arithmetic  12.9 us (5%)
  waiting for transfers between devices  9.12 us (4%)
  local copies, waits for them, and re-layouts  2.89 us (1%)
    all_gather x1, blocking collectives, body(): kpiece = lax.all_gather(prefix_cached_keys[0], 'ctx', axis=0, tiled=True)  78.8 us
    all_gather x1, blocking collectives, body(): vpiece = lax.all_gather(prefix_cached_values[0], 'ctx', axis=0, tiled=True)  65.9 us
    ppermute x2, starting transfers between devices, partner(): lax.ppermute(value, axis, [(i, i ^ 1 << apart) for i in range(lax.axis_si...  31 us
    dot_general x2, matrix products, softmax_update(): jnp.einsum('kgqn,nkd->kgqd', probs, vals, preferred_element_type=jnp.floa...  7.83 us
    all_gather x1, waiting for transfers between devices, body(): lax.all_gather(fresh_token_values[0], 'ctx', axis=0, tiled=True)  7.7 us
    reduce_sum x2, other arithmetic, softmax_update(): total = total * factor + jnp.sum(weights, axis=-1)  6.72 us
    dot_general x2, matrix products, softmax_update(): jnp.einsum('qkgd,nkd->kgqn', query_heads, keys, preferred_element_type=jn...  5.02 us
    dot_general x2, matrix products, pick_rows(): jnp.dot(onehot.astype(jnp.bfloat16), piece, preferred_element_type=jnp.fl...  4.93 us
  transfers between devices with their start and end apart: 6, of which 1 were waited for; matrix products, arithmetic and copies ran while one was open for 13% of the time, Pallas kernels for 0%

commit v1 on v0

v1 whole, which is shorter than its diff:
```python
import functools
import math

import jax
import jax.numpy as jnp
from jax import lax
from jax.experimental import pallas as pl
from jax.experimental.pallas import tpu as pltpu
from jax.sharding import Mesh, PartitionSpec as P

HEAD = 128
PAGE = 16
HEADS = 8
NEW = 128
OLD = 64
ROWS = 2 * NEW + 2 * OLD
Z, Y = 4, 8
STEP_NEW, STEP_OLD = Z * NEW, Z * OLD
SCALE = 1.0 / math.sqrt(HEAD) * math.log2(math.e)


def shift(value, axes, apart, sizes):
    count = math.prod(sizes)

    def moved(i):
        at, out = [], 0
        for size in reversed(sizes):
            at.append(i % size)
            i //= size
        for place, step, size in zip(reversed(at), apart, sizes):
            out = out * size + (place + step) % size
        return out

    return lax.ppermute(value, axes, [(i, moved(i)) for i in range(count)])


def attend_kernel(scal, q_ref, kv_ref, o_ref, m_ref, acc_ref):
    j = pl.program_id(0)
    ctx, length, prefix = scal[0], scal[1], scal[2]
    y = lax.div(ctx, Z)
    width = STEP_NEW + STEP_OLD
    tile = 256
    heads = tile // NEW

    @pl.when(j == 0)
    def _():
        m_ref[...] = jnp.full(m_ref.shape, -1e30, jnp.float32)
        acc_ref[...] = jnp.zeros(acc_ref.shape, jnp.float32)

    def step(masked):
        k = jnp.concatenate(
            [kv_ref[z, 0:NEW, :] for z in range(Z)]
            + [kv_ref[z, 2 * NEW : 2 * NEW + OLD, :] for z in range(Z)],
            axis=0,
        )
        v = jnp.concatenate(
            [kv_ref[z, NEW : 2 * NEW, :] for z in range(Z)]
            + [kv_ref[z, 2 * NEW + OLD : ROWS, :] for z in range(Z)],
            axis=0,
        )
        v = jnp.concatenate([v, jnp.ones_like(v)], axis=1)
        for t in range(HEADS // heads):
            q = jnp.concatenate(
                [q_ref[:, (t * heads + i) * HEAD : (t * heads + i + 1) * HEAD] for i in range(heads)],
                axis=0,
            )
            s = lax.dot_general(q, k, (((1,), (1,)), ((), ())), preferred_element_type=jnp.float32)
            if masked:
                col = lax.broadcasted_iota(jnp.int32, (tile, width), 1)
                row = lax.broadcasted_iota(jnp.int32, (tile, width), 0) & (NEW - 1)
                new = col < STEP_NEW
                place = jnp.where(new, col + j * STEP_NEW, col - STEP_NEW + j * STEP_OLD)
                limit = jnp.where(new, row + (ctx * NEW + 1), prefix)
                s = jnp.where(place < limit, s, -1e30)
            r = pl.ds(t * tile, tile)
            old = m_ref[r, :]
            top = jnp.maximum(old, jnp.max(s, axis=1, keepdims=True))
            p = jnp.exp2((s - top[:, :1]) * SCALE)
            factor = jnp.exp2((old - top) * SCALE)
            m_ref[r, :] = top
            pv = jnp.dot(p.astype(jnp.bfloat16), v, preferred_element_type=jnp.float32)
            acc_ref[r, :] = acc_ref[r, :] * jnp.concatenate([factor, factor], axis=1) + pv

    live = ctx * NEW < length
    full = (j < y) & ((j + 1) * STEP_OLD <= prefix)
    some = (j <= y) | (j * STEP_OLD < prefix)

    @pl.when(live & full)
    def _():
        step(False)

    @pl.when(live & some & jnp.logical_not(full))
    def _():
        step(True)

    @pl.when(j == pl.num_programs(0) - 1)
    def _():
        row = lax.broadcasted_iota(jnp.int32, (NEW, HEAD), 0) + ctx * NEW
        for h in range(HEADS):
            a = acc_ref[pl.ds(h * NEW, NEW), :]
            o = a[:, :HEAD] / a[:, HEAD:]
            o_ref[:, h * HEAD : (h + 1) * HEAD] = jnp.where(row < length, o, 0.0).astype(jnp.bfloat16)


def attend(scal, q, kv):
    return pl.pallas_call(
        attend_kernel,
        grid_spec=pltpu.PrefetchScalarGridSpec(
            num_scalar_prefetch=1,
            grid=(Y,),
            in_specs=[
                pl.BlockSpec((NEW, HEADS * HEAD), lambda j, s: (0, 0)),
                pl.BlockSpec((Z, ROWS, HEAD), lambda j, s: (j, 0, 0)),
            ],
            out_specs=pl.BlockSpec((NEW, HEADS * HEAD), lambda j, s: (0, 0)),
            scratch_shapes=[
                pltpu.VMEM((HEADS * NEW, HEAD), jnp.float32),
                pltpu.VMEM((HEADS * NEW, 2 * HEAD), jnp.float32),
            ],
        ),
        out_shape=jax.ShapeDtypeStruct((NEW, HEADS * HEAD), jnp.bfloat16),
        compiler_params=pltpu.CompilerParams(vmem_limit_bytes=40 << 20),
        cost_estimate=pl.CostEstimate(
            flops=4 * HEADS * NEW * Y * (STEP_NEW + STEP_OLD) * HEAD,
            bytes_accessed=4 << 20,
            transcendentals=HEADS * NEW * Y * (STEP_NEW + STEP_OLD),
        ),
        name="attend",
    )(scal, q, kv)


PAGES = Z * NEW // PAGE


def place_kernel(scal, slots, kv_ref, o_ref):
    ctx, length = scal[0], scal[1]
    y, z = lax.div(ctx, Z), lax.rem(ctx, Z)
    o_ref[...] = jnp.zeros(o_ref.shape, jnp.bfloat16)
    row = lax.broadcasted_iota(jnp.int32, (PAGE, HEAD), 0)
    for page in range(PAGES):
        slot = slots[y * PAGES + page]
        at = lax.div(slot, 8)
        src, first = page * PAGE // NEW, page * PAGE % NEW

        @pl.when(lax.rem(at, Z) == z)
        def _():
            to = lax.div(at, Z) * 8 + lax.rem(slot, 8)
            keep = row < length - (y * PAGES + page) * PAGE
            for half in range(2):
                rows = kv_ref[src, half * NEW + first : half * NEW + first + PAGE, :]
                rows = jnp.where(keep, rows.astype(jnp.float32), 0.0).astype(jnp.bfloat16)
                o_ref[to, half * PAGE : (half + 1) * PAGE, :] = rows


def place(scal, slots, kv, tps):
    return pl.pallas_call(
        place_kernel,
        grid_spec=pltpu.PrefetchScalarGridSpec(
            num_scalar_prefetch=2,
            grid=(1,),
            in_specs=[pl.BlockSpec((Z, 2 * NEW, HEAD), lambda j, s, t: (0, 0, 0))],
            out_specs=pl.BlockSpec((Y * tps, 2 * PAGE, HEAD), lambda j, s, t: (0, 0, 0)),
        ),
        out_shape=jax.ShapeDtypeStruct((Y * tps, 2 * PAGE, HEAD), jnp.bfloat16),
        compiler_params=pltpu.CompilerParams(vmem_limit_bytes=16 << 20),
        name="place_pages",
    )(scal, slots, kv)


def body(q, new_k, new_v, old_k, old_v, prompt_len, prefix_len, slots):
    ctx = lax.axis_index(("y", "zh")).astype(jnp.int32)
    tp = lax.axis_index(("x", "zl")).astype(jnp.int32)
    tps = lax.axis_size(("x", "zl"))
    scal = jnp.stack([ctx, prompt_len[0], prefix_len[0]])
    slots = slots[0]
    mine = jnp.concatenate([new_k[0], new_v[0], old_k[0], old_v[0]], axis=0)
    column = lax.all_gather(mine, "zh", axis=0)
    everything = lax.all_gather(column, "y", axis=0, tiled=True)

    sent = place(scal, slots, column, tps)
    got = lax.all_to_all(sent, ("y", "x", "zl"), split_axis=0, concat_axis=0, tiled=True)
    page = jnp.sum(jnp.where(slots == ctx * tps + tp, jnp.arange(slots.shape[0], dtype=jnp.int32), 0))
    from_y = lax.div(page, jnp.int32(PAGES))
    got = got.reshape(Y, tps, 2 * PAGE, HEAD)
    got = lax.dynamic_index_in_dim(got, from_y, 0, keepdims=False)
    got = shift(got, "core", (1,), (2,))
    got = got.transpose(1, 0, 2).reshape(2 * PAGE, tps * HEAD)
    out = attend(scal, q[0], everything)
    return out[None], got[None, :PAGE], got[None, PAGE:]


def solution(mesh):
    grid = Mesh(mesh.devices.reshape(Y, Z, 4, 2, 2), ("y", "zh", "x", "zl", "core"))
    ctx, tp = ("y", "zh"), ("x", "zl")
    split = P("core", ctx, tp)
    in_specs = (split, split, split, split, split, P("core"), P("core"), P("core", None))
    out_specs = (split, P("core", ctx + tp, None), P("core", ctx + tp, None))
    return jax.shard_map(body, mesh=grid, in_specs=in_specs, out_specs=out_specs, check_vma=False)
```

time: 244 us -> 112 us (0.46)
  blocking collectives: 145 us -> 20.3 us
  waiting for transfers between devices: 9.12 us -> 32.5 us
  starting transfers between devices: 39.7 us -> 17.8 us
  matrix products: 17.8 us -> 0 us
  Pallas kernels: 0 us -> 16.7 us
  other arithmetic: 12.9 us -> 2.24 us
    all_gather x2 -> x1, blocking collectives: 145 us -> 20.3 us  [body(): column = lax.all_gather(mine, 'zh', axis=0)]
    ppermute x2 -> x1, starting transfers between devices: 31 us -> 6.49 us  [shift(): return lax.ppermute(value, axes, [(i, moved(i)) for i in range(count)])]
    dot_general x6 -> x0, matrix products: 17.8 us -> none  [the longest x2 7.83 us: softmax_update(): jnp.einsum('kgqn,nkd->kgqd', probs, vals, preferred_element_type=jnp.floa...]
    all_to_all x2 -> x1, waiting for transfers between devices: 0.01 us -> 17.4 us  [body(): lax.all_to_all(sent, ('y', 'x', 'zl'), split_axis=0, concat_axis=0, tiled...]
    pallas_call x0 -> x2, Pallas kernels: none -> 16.7 us  [the longest x1 14.8 us: attend(): pl.pallas_call(attend_kernel, grid_spec=pltpu.PrefetchScalarGridSpec(num_...]
    all_gather x2 -> x1, waiting for transfers between devices: 7.72 us -> 14.1 us  [body(): everything = lax.all_gather(column, 'y', axis=0, tiled=True)]
    reduce_sum x3 -> x1, other arithmetic: 7.58 us -> 1.32 us  [body(): jnp.sum(jnp.where(slots == ctx * tps + tp, jnp.arange(slots.shape[0], dty...]
    all_to_all x2 -> x1, starting transfers between devices: 8.62 us -> 11.3 us  [body(): lax.all_to_all(sent, ('y', 'x', 'zl'), split_axis=0, concat_axis=0, tiled...]
  transfers between devices with their start and end apart: 6 -> 3, of which waited for: 1 -> 3; matrix products, arithmetic and copies ran while one was open for 13% -> 2% of each run, Pallas kernels for 0% -> 2%
where the time goes in v1:
time: 112 us
  waiting for transfers between devices  32.5 us (29%)
  blocking collectives  20.3 us (18%)
  starting transfers between devices  17.8 us (16%)
  between operations  17.3 us (15%)
  Pallas kernels  16.7 us (15%)
  local copies, waits for them, and re-layouts  4.87 us (4%)
  other arithmetic  2.24 us (2%)
    all_gather x1, blocking collectives, body(): column = lax.all_gather(mine, 'zh', axis=0)  20.3 us
    all_to_all x1, waiting for transfers between devices, body(): lax.all_to_all(sent, ('y', 'x', 'zl'), split_axis=0, concat_axis=0, tiled...  17.4 us
    pallas_call x1, Pallas kernels, attend(): pl.pallas_call(attend_kernel, grid_spec=pltpu.PrefetchScalarGridSpec(num_...  14.8 us
    all_gather x1, waiting for transfers between devices, body(): everything = lax.all_gather(column, 'y', axis=0, tiled=True)  14.1 us
    all_to_all x1, starting transfers between devices, body(): lax.all_to_all(sent, ('y', 'x', 'zl'), split_axis=0, concat_axis=0, tiled...  11.3 us
    ppermute x1, starting transfers between devices, shift(): return lax.ppermute(value, axes, [(i, moved(i)) for i in range(count)])  6.49 us
    unnamed x8, local copies, waits for them, and re-layouts  3.57 us
  transfers between devices with their start and end apart: 3, of which 3 were waited for; matrix products, arithmetic and copies ran while one was open for 2% of the time, Pallas kernels for 2%

profile of v1, /device:TPU:1, one launch (start us, length us, event | category | flops | bytes accessed | tf_op | source)
XLA Modules:
  0.0 111.8 jit_solution(8856451839775567638)
XLA Ops:
  7.2 0.0 copy-start.3
  7.2 0.0 all-gather.3.cloned.1.call-start
  7.2 0.8 pad_maximum_fusion
  8.1 20.3 %all-gather = bf16[1536,128]{1,0:T(8,128)(2,1)} all-gather(bf16[384,128]{1,0:T(8,128)(2,1)S(1)} %pad_maximum_fusion), channel_id=2, replica_groups=mesh['y'=8,'zh'=4,'x'=4,'zl'=2,'core'=2] {'zh'}, dimensions={0}, use_global_device_ids=true | all-gather | bytes 491520 | tf_op jit(solution)/shard_map/all_gather | solution.py:177
  28.4 0.0 all-gather.3.cloned.1.call-update
  29.7 0.1 pad_add_fusion.scal
  29.8 0.0 copy-start
  29.8 1.0 copy-done
  30.8 0.0 copy-start.1
  30.8 0.7 copy-done.1
  31.5 1.9 %place_pages.1 = bf16[64,32,128]{2,1,0:T(8,128)(2,1)} custom-call(s32[3]{0:T(128)S(1)} %pad_add_fusion.scal, s32[256]{0:T(256)S(1)} %bitcast.16, bf16[4,384,128]{2,1,0:T(8,128)(2,1)S(1)} %bitcast.14), custom_call_target="tpu_custom_call" | custom-call | tf_op jit(solution)/shard_map/place_pages/pallas_call | solution.py:156
  33.4 11.3 %all-to-all-start = ((bf16[64,32,128]{2,1,0:T(8,128)(2,1)}), bf16[64,32,128]{2,1,0:T(8,128)(2,1)S(1)}, u32[]{:S(2)}, u32[]{:S(2)}) async-start(bf16[64,32,128]{2,1,0:T(8,128)(2,1)} %place_pages.1), calls=%async_computation | async-start | bytes 1048576 | tf_op jit(solution)/shard_map/all_to_all | solution.py:181
  44.7 1.3 %fusion = s32[]{:T(128)} fusion(s32[256]{0:T(256)} %bitcast.15, s32[]{:T(128)S(6)} %add.15), kind=kLoop, calls=%fused_computation.3 | loop fusion | flops 767 | bytes 1032 | tf_op jit(solution)/shard_map/reduce_sum | solution.py:182
  48.0 17.4 %all-to-all-done = bf16[64,32,128]{2,1,0:T(8,128)(2,1)S(1)} async-done(((bf16[64,32,128]{2,1,0:T(8,128)(2,1)}), bf16[64,32,128]{2,1,0:T(8,128)(2,1)S(1)}, u32[]{:S(2)}, u32[]{:S(2)}) %all-to-all-start) | async-done | bytes 524320 | tf_op jit(solution)/shard_map/all_to_all | solution.py:181
  65.4 6.5 %collective-permute-start = (bf16[8,32,128]{2,1,0:T(8,128)(2,1)S(1)}, bf16[8,32,128]{2,1,0:T(8,128)(2,1)S(1)}, u32[]{:S(2)}, u32[]{:S(2)}) collective-permute-start(bf16[8,32,128]{2,1,0:T(8,128)(2,1)S(1)} %dynamic-slice_bitcast_fusion), channel_id=1, source_target_pairs={{0,1},{1,0},{2,3},{3,2},{4,5},{5,4},{6,7},{7,6},{8,9},{9,8},{10,11... | collective-permute-start | bytes 196616 | tf_op jit(solution)/shard_map/ppermute | solution.py:34
  71.9 0.9 collective-permute-done
  72.8 0.6 broadcast_in_dim.15
  73.5 0.6 broadcast_in_dim.16
  74.1 14.1 %all-gather.3.cloned.1.call-done.kv_ref = bf16[32,384,128]{2,1,0:T(8,128)(2,1)} async-done(((bf16[4,384,128]{2,1,0:T(8,128)(2,1)}), bf16[32,384,128]{2,1,0:T(8,128)(2,1)}) %all-gather.3.cloned.1.call-update) | async-done | bytes 3145744 | tf_op jit(solution)/shard_map/all_gather | solution.py:178
  88.3 0.0 copy-done.3
  88.3 0.0 copy-start.2
  88.3 1.9 %copy-done.2 = bf16[32,384,128]{2,1,0:T(8,128)(2,1)S(1)} copy-done((bf16[32,384,128]{2,1,0:T(8,128)(2,1)S(1)}, bf16[32,384,128]{2,1,0:T(8,128)(2,1)}, u32[]{:S(2)}) %copy-start.2) | copy-done | bytes 3145752
  90.1 14.8 %attend.1 = bf16[128,1024]{1,0:T(8,128)(2,1)} custom-call(s32[3]{0:T(128)S(1)} %pad_add_fusion.scal, bf16[128,1024]{1,0:T(8,128)(2,1)S(1)} %bitcast.17, bf16[32,384,128]{2,1,0:T(8,128)(2,1)S(1)} %copy-done.2), custom_call_target="tpu_custom_call" | custom-call | flops 3221225472 | bytes 4194304 | tf_op jit(solution)/shard_map/attend/pallas_call | solution.py:106
  (4 shorter events, 0.0 us)
Async XLA Ops:
  7.2 81.1 %copy-start.3 = (bf16[1,128,1024]{2,1,0:T(8,128)(2,1)S(1)}, bf16[1,128,1024]{2,1,0:T(8,128)(2,1)}, u32[]{:S(2)}) copy-start(bf16[1,128,1024]{2,1,0:T(8,128)(2,1)} %param.8) | copy-start | bytes 786436
  7.2 81.1 %all-gather.3.cloned.1.call-start = ((), (), s32[]{:S(2)}) async-start(), calls=%async_computation.1 | async-start | bytes 3538944 | tf_op jit(solution)/shard_map/all_gather | solution.py:178
  29.8 1.0 copy-start
  30.8 0.7 copy-start.1
  33.4 32.1 %all-to-all-start = ((bf16[64,32,128]{2,1,0:T(8,128)(2,1)}), bf16[64,32,128]{2,1,0:T(8,128)(2,1)S(1)}, u32[]{:S(2)}, u32[]{:S(2)}) async-start(bf16[64,32,128]{2,1,0:T(8,128)(2,1)} %place_pages.1), calls=%async_computation | async-start | bytes 1048576 | tf_op jit(solution)/shard_map/all_to_all | solution.py:181
  65.4 7.4 %collective-permute-start = (bf16[8,32,128]{2,1,0:T(8,128)(2,1)S(1)}, bf16[8,32,128]{2,1,0:T(8,128)(2,1)S(1)}, u32[]{:S(2)}, u32[]{:S(2)}) collective-permute-start(bf16[8,32,128]{2,1,0:T(8,128)(2,1)S(1)} %dynamic-slice_bitcast_fusion), channel_id=1, source_target_pairs={{0,1},{1,0},{2,3},{3,2},{4,5},{5,4},{6,7},{7,6},{8,9},{9,8},{10,11... | collective-permute-start | bytes 196616 | tf_op jit(solution)/shard_map/ppermute | solution.py:34
  88.3 1.9 %copy-start.2 = (bf16[32,384,128]{2,1,0:T(8,128)(2,1)S(1)}, bf16[32,384,128]{2,1,0:T(8,128)(2,1)}, u32[]{:S(2)}) copy-start(bf16[32,384,128]{2,1,0:T(8,128)(2,1)} %all-gather.3.cloned.1.call-done.kv_ref) | copy-start | bytes 9437188
Sparse Core Ops, SparseCore 0:
  28.5 59.6 all-gather.2

commit v2 on v1

v2 whole, which is shorter than its diff:
```python
import functools
import math

import jax
import jax.numpy as jnp
from jax import lax
from jax.experimental import pallas as pl
from jax.experimental.pallas import tpu as pltpu
from jax.sharding import Mesh, PartitionSpec as P

HEAD = 128
PAGE = 16
HEADS = 8
NEW = 128
OLD = 64
ROWS = 2 * NEW + 2 * OLD
Z, Y = 4, 8
STEP_NEW, STEP_OLD = Z * NEW, Z * OLD
COST = 40
SCALE = 1.0 / math.sqrt(HEAD) * math.log2(math.e)


def shift(value, axes, apart, sizes):
    count = math.prod(sizes)

    def moved(i):
        at, out = [], 0
        for size in reversed(sizes):
            at.append(i % size)
            i //= size
        for place, step, size in zip(reversed(at), apart, sizes):
            out = out * size + (place + step) % size
        return out

    return lax.ppermute(value, axes, [(i, moved(i)) for i in range(count)])


def attend_kernel(scal, q_ref, *refs, apart, first, last):
    count = len(apart)
    blocks, refs = refs[:count], refs[count:]
    if not first:
        m_ref, acc_ref, *refs = refs
    o_ref = None
    if last:
        o_ref, *refs = refs
    elif first:
        m_ref, acc_ref, *refs = refs
    else:
        m_ref, acc_ref, *refs = refs
    held, arrived = refs
    copies = [pltpu.make_async_copy(blocks[i], held.at[i], arrived.at[i]) for i in range(count)]
    for copy in copies:
        copy.start()
    if first:
        m_ref[...] = jnp.full(m_ref.shape, -1e30, jnp.float32)
        acc_ref[...] = jnp.zeros(acc_ref.shape, jnp.float32)
    ctx, length, prefix = scal[0], scal[1], scal[2]
    y = lax.div(ctx, Z)
    live = ctx * NEW < length
    tile = 256
    heads = tile // NEW

    def step(i, j, masked, with_new=True):
        new_keys = STEP_NEW if with_new else 0
        width = new_keys + STEP_OLD
        k = [held[i, z, 0:NEW, :] for z in range(Z)] if with_new else []
        k += [held[i, z, 2 * NEW : 2 * NEW + OLD, :] for z in range(Z)]
        v = [held[i, z, NEW : 2 * NEW, :] for z in range(Z)] if with_new else []
        v += [held[i, z, 2 * NEW + OLD : ROWS, :] for z in range(Z)]
        k, v = jnp.concatenate(k, axis=0), jnp.concatenate(v, axis=0)
        v = jnp.concatenate([v, jnp.ones_like(v)], axis=1)

        def scores(t):
            q = jnp.concatenate(
                [q_ref[:, (t * heads + n) * HEAD : (t * heads + n + 1) * HEAD] for n in range(heads)],
                axis=0,
            )
            s = lax.dot_general(q, k, (((1,), (1,)), ((), ())), preferred_element_type=jnp.float32)
            if masked:
                col = lax.broadcasted_iota(jnp.int32, (tile, width), 1)
                row = lax.broadcasted_iota(jnp.int32, (tile, width), 0) & (NEW - 1)
                new = col < new_keys
                place = jnp.where(new, col + j * STEP_NEW, col - new_keys + j * STEP_OLD)
                limit = jnp.where(new, row + (ctx * NEW + 1), prefix)
                s = jnp.where(place < limit, s, -1e30)
            return s

        s = scores(0)
        for t in range(HEADS // heads):
            ahead = scores(t + 1) if t + 1 < HEADS // heads else None
            r = pl.ds(t * tile, tile)
            old = m_ref[r, :]
            top = jnp.maximum(old, jnp.max(s, axis=1, keepdims=True))
            p = jnp.exp2((s - top[:, :1]) * SCALE)
            factor = jnp.exp2((old - top) * SCALE)
            m_ref[r, :] = top
            pv = jnp.dot(p.astype(jnp.bfloat16), v, preferred_element_type=jnp.float32)
            acc_ref[r, :] = acc_ref[r, :] * jnp.concatenate([factor, factor], axis=1) + pv
            s = ahead

    for i, far in enumerate(apart):
        copies[i].wait()
        j = lax.rem(y + far + Y, Y)
        old_full = (j + 1) * STEP_OLD <= prefix
        old_some = j * STEP_OLD < prefix
        if far == 0:
            pl.when(live)(functools.partial(step, i, j, True))
        else:
            pl.when(live & (j < y) & old_full)(functools.partial(step, i, j, False))
            pl.when(live & (j < y) & jnp.logical_not(old_full))(functools.partial(step, i, j, True))
            pl.when(live & (j > y) & old_some)(functools.partial(step, i, j, True, False))

    if last:
        row = lax.broadcasted_iota(jnp.int32, (NEW, HEAD), 0) + ctx * NEW
        for h in range(HEADS):
            a = acc_ref[pl.ds(h * NEW, NEW), :]
            o = a[:, :HEAD] / a[:, HEAD:]
            o_ref[:, h * HEAD : (h + 1) * HEAD] = jnp.where(row < length, o, 0.0).astype(jnp.bfloat16)


def attend(scal, q, blocks, apart, state=None, last=False):
    whole = pl.BlockSpec(memory_space=pltpu.VMEM)
    saved = (
        jax.ShapeDtypeStruct((HEADS * NEW, HEAD), jnp.float32),
        jax.ShapeDtypeStruct((HEADS * NEW, 2 * HEAD), jnp.float32),
    )
    first, count = state is None, len(apart)
    keys = count * (STEP_NEW + STEP_OLD)
    return pl.pallas_call(
        functools.partial(attend_kernel, apart=apart, first=first, last=last),
        in_specs=[pl.BlockSpec(memory_space=pltpu.SMEM), whole]
        + [pl.BlockSpec(memory_space=pl.ANY)] * count
        + ([] if first else [whole] * 2),
        out_specs=whole if last else (whole, whole),
        out_shape=jax.ShapeDtypeStruct((NEW, HEADS * HEAD), jnp.bfloat16) if last else saved,
        input_output_aliases={} if first or last else {2 + count: 0, 3 + count: 1},
        scratch_shapes=[
            pltpu.VMEM((count, Z, ROWS, HEAD), jnp.bfloat16),
            pltpu.SemaphoreType.DMA((count,)),
        ],
        compiler_params=pltpu.CompilerParams(vmem_limit_bytes=32 << 20),
        cost_estimate=pl.CostEstimate(
            flops=COST * HEADS * NEW * keys * HEAD,
            bytes_accessed=count * Z * ROWS * HEAD * 2,
            transcendentals=HEADS * NEW * keys,
        ),
        name="attend_blocks",
    )(scal, q, *blocks, *(() if first else state))


PAGES = Z * NEW // PAGE


def pick_kernel(scal, pages, *refs):
    blocks, (o_ref, held, arrived) = refs[:Y], refs[Y:]
    y, length = lax.div(scal[0], Z), scal[1]
    count = held.shape[0]
    for k in range(count):
        page = pages[k]
        away = lax.rem(lax.div(page, PAGES) - y + Y, Y)
        inside = lax.rem(page, PAGES)
        z = lax.div(inside, NEW // PAGE)
        first = pl.multiple_of(lax.rem(inside, NEW // PAGE) * PAGE, PAGE)
        for d in range(Y):

            @pl.when(away == d)
            def _():
                for half in range(2):
                    pltpu.make_async_copy(
                        blocks[d].at[z, pl.ds(half * NEW + first, PAGE)],
                        held.at[k, pl.ds(half * PAGE, PAGE)],
                        arrived.at[k, half],
                    ).start()

    row = lax.broadcasted_iota(jnp.int32, (PAGE, HEAD), 0)
    for k in range(count):
        keep = row < length - pages[k] * PAGE
        for half in range(2):
            rows = pl.ds(half * PAGE, PAGE)
            pltpu.make_async_copy(
                blocks[0].at[0, pl.ds(0, PAGE)], held.at[k, rows], arrived.at[k, half]
            ).wait()
            page = jnp.where(keep, held[k, rows, :].astype(jnp.float32), 0.0).astype(jnp.bfloat16)
            for core in range(2):
                o_ref[k, core, rows, :] = page


def pick(scal, pages, blocks):
    count = pages.shape[0]
    small = pl.BlockSpec(memory_space=pltpu.SMEM)
    return pl.pallas_call(
        pick_kernel,
        in_specs=[small, small] + [pl.BlockSpec(memory_space=pl.ANY)] * Y,
        out_specs=pl.BlockSpec(memory_space=pltpu.VMEM),
        out_shape=jax.ShapeDtypeStruct((count, 2, 2 * PAGE, HEAD), jnp.bfloat16),
        scratch_shapes=[
            pltpu.VMEM((count, 2 * PAGE, HEAD), jnp.bfloat16),
            pltpu.SemaphoreType.DMA((count, 2)),
        ],
        name="pick_pages",
    )(scal, pages, *blocks)


def assemble_kernel(core, got_ref, k_ref, v_ref):
    other = 1 - core[0]
    for t in range(got_ref.shape[0]):
        for half, out in enumerate((k_ref, v_ref)):
            out[0, :, t * HEAD : (t + 1) * HEAD] = got_ref[t, other, half * PAGE : (half + 1) * PAGE, :]


def assemble(core, got):
    tps = got.shape[0]
    whole = pl.BlockSpec(memory_space=pltpu.VMEM)
    return pl.pallas_call(
        assemble_kernel,
        in_specs=[pl.BlockSpec(memory_space=pltpu.SMEM), whole],
        out_specs=(whole, whole),
        out_shape=(jax.ShapeDtypeStruct((1, PAGE, tps * HEAD), jnp.bfloat16),) * 2,
        name="assemble_pages",
    )(core, got)


def farthest(right, left):
    core = lax.axis_index("core")
    pairs = []
    for i in range(2 * Y):
        y, c = i // 2, i % 2
        pairs.append((i, (y + (1 if c == 0 else -1)) % Y * 2 + c))
    return lax.ppermute(jnp.where(core == 0, right, left), ("y", "core"), pairs)


def body(q, new_k, new_v, old_k, old_v, prompt_len, prefix_len, slots):
    ctx = lax.axis_index(("y", "zh")).astype(jnp.int32)
    core = lax.axis_index("core").astype(jnp.int32)
    tps = lax.axis_size(("x", "zl"))
    scal = jnp.stack([ctx, prompt_len[0], prefix_len[0]])
    mine = jnp.concatenate([new_k[0], new_v[0], old_k[0], old_v[0]], axis=0)
    column = lax.all_gather(mine, "zh", axis=0)
    right, left = [column], [column]
    for _ in range(3):
        right.append(shift(right[-1], ("y",), (1,), (Y,)))
        left.append(shift(left[-1], ("y",), (-1,), (Y,)))
    far = farthest(right[3], left[3])

    slots_here = ctx * tps + jnp.arange(tps, dtype=jnp.int32)
    page_ids = jnp.arange(slots.shape[1], dtype=jnp.int32)
    pages = jnp.sum(jnp.where(slots[0][None, :] == slots_here[:, None], page_ids[None, :], 0), axis=1)
    by_distance = [column, left[1], left[2], left[3], far, right[3], right[2], right[1]]
    sent = pick(scal, pages, by_distance).reshape(2 * tps, 2 * PAGE, HEAD)
    got = lax.all_to_all(sent, ("x", "zl", "core"), split_axis=0, concat_axis=0, tiled=True)
    pools = assemble(core[None], got.reshape(tps, 2, 2 * PAGE, HEAD))

    state = attend(scal, q[0], [column], (0,))
    for away in (1, 2, 3):
        state = attend(scal, q[0], [right[away], left[away]], (-away, away), state)
    out = attend(scal, q[0], [far], (4,), state, last=True)
    return (out[None], *pools)


def solution(mesh):
    grid = Mesh(mesh.devices.reshape(Y, Z, 4, 2, 2), ("y", "zh", "x", "zl", "core"))
    ctx, tp = ("y", "zh"), ("x", "zl")
    split = P("core", ctx, tp)
    in_specs = (split, split, split, split, split, P("core"), P("core"), P("core", None))
    out_specs = (split, P("core", ctx + tp, None), P("core", ctx + tp, None))
    return jax.shard_map(body, mesh=grid, in_specs=in_specs, out_specs=out_specs, check_vma=False)
```

time: 112 us -> 92.5 us (0.83)
  waiting for transfers between devices: 32.5 us -> 9.77 us
  starting transfers between devices: 17.8 us -> 35.9 us
  between operations: 17.3 us -> 2.22 us
    all_to_all x1, waiting for transfers between devices: 17.4 us -> 2.04 us  [body(): lax.all_to_all(sent, ('x', 'zl', 'core'), split_axis=0, concat_axis=0, ti...]
    ppermute x1 -> x6, starting transfers between devices: 6.49 us -> 20.7 us  [shift(): return lax.ppermute(value, axes, [(i, moved(i)) for i in range(count)])]
    all_gather x1 -> x0, waiting for transfers between devices: 14.1 us -> none  [body(): everything = lax.all_gather(column, 'y', axis=0, tiled=True)]
    ppermute x1 -> x6, waiting for transfers between devices: 0.88 us -> 5.19 us  [shift(): return lax.ppermute(value, axes, [(i, moved(i)) for i in range(count)])]
    ppermute x0 -> x1, waiting for transfers between devices: none -> 2.54 us  [farthest(): return lax.ppermute(jnp.where(core == 0, right, left), ('y', 'core'), pairs)]
    all_to_all x1, starting transfers between devices: 11.3 us -> 13.3 us  [body(): lax.all_to_all(sent, ('x', 'zl', 'core'), split_axis=0, concat_axis=0, ti...]
    ppermute x0 -> x1, starting transfers between devices: none -> 1.92 us  [farthest(): return lax.ppermute(jnp.where(core == 0, right, left), ('y', 'core'), pairs)]
    broadcast_in_dim x2 -> x0, local copies, waits for them, and re-layouts: 1.27 us -> none  [body(): return (out[None], got[None, :PAGE], got[None, PAGE:])]
  transfers between devices with their start and end apart: 3 -> 8, of which waited for: 3 -> 4; matrix products, arithmetic and copies ran while one was open for 2% -> 1% of each run, Pallas kernels for 2% -> 15%
where the time goes in v2:
time: 92.5 us; the launch traced here: 91.9 us
  starting transfers between devices  35.9 us (39%)
  blocking collectives  20 us (22%)
  Pallas kernels  17.6 us (19%)
  waiting for transfers between devices  9.77 us (11%)
  local copies, waits for them, and re-layouts  4.76 us (5%)
  between operations  2.22 us (2%)
  other arithmetic  1.63 us (2%)
    ppermute x6, starting transfers between devices, shift(): return lax.ppermute(value, axes, [(i, moved(i)) for i in range(count)])  20.7 us
    all_gather x1, blocking collectives, body(): column = lax.all_gather(mine, 'zh', axis=0)  20 us
    pallas_call x5, Pallas kernels, attend(): pl.pallas_call(functools.partial(attend_kernel, apart=apart, first=first,...  13.5 us
    all_to_all x1, starting transfers between devices, body(): lax.all_to_all(sent, ('x', 'zl', 'core'), split_axis=0, concat_axis=0, ti...  13.3 us
    ppermute x6, waiting for transfers between devices, shift(): return lax.ppermute(value, axes, [(i, moved(i)) for i in range(count)])  5.19 us
    unnamed x32, local copies, waits for them, and re-layouts  4.76 us
    ppermute x1, waiting for transfers between devices, farthest(): return lax.ppermute(jnp.where(core == 0, right, left), ('y', 'core'), pairs)  2.54 us
    pallas_call x1, Pallas kernels, pick(): pl.pallas_call(pick_kernel, in_specs=[small, small] + [pl.BlockSpec(memor...  2.49 us
  transfers between devices with their start and end apart: 8, of which 4 were waited for; matrix products, arithmetic and copies ran while one was open for 1% of the time, Pallas kernels for 15%

profile of v2, /device:TPU:1, one launch (start us, length us, event | category | flops | bytes accessed | tf_op | source)
XLA Modules:
  0.0 91.9 jit_solution(14570628867140765098)
XLA Ops:
  0.6 0.8 pad_maximum_fusion
  1.5 20.0 %all-gather = bf16[1536,128]{1,0:T(8,128)(2,1)S(1)} all-gather(bf16[384,128]{1,0:T(8,128)(2,1)S(1)} %pad_maximum_fusion), channel_id=2, replica_groups=mesh['y'=8,'zh'=4,'x'=4,'zl'=2,'core'=2] {'zh'}, dimensions={0}, use_global_device_ids=true | all-gather | bytes 491520 | tf_op jit(solution)/shard_map/all_gather | solution.py:238
  21.5 5.1 %collective-permute-start.3 = (bf16[4,384,128]{2,1,0:T(8,128)(2,1)S(1)}, bf16[4,384,128]{2,1,0:T(8,128)(2,1)S(1)}, u32[]{:S(2)}, u32[]{:S(2)}) collective-permute-start(bf16[4,384,128]{2,1,0:T(8,128)(2,1)S(1)} %bitcast.12), channel_id=1, source_target_pairs={{0,448},{64,0},{128,64},{192,128},{256,192},{320,256},{384,320},{4... | collective-permute-start | bytes 1179656 | tf_op jit(solution)/shard_map/ppermute | solution.py:35
  26.6 1.9 %collective-permute-start = (bf16[4,384,128]{2,1,0:T(8,128)(2,1)S(1)}, bf16[4,384,128]{2,1,0:T(8,128)(2,1)S(1)}, u32[]{:S(2)}, u32[]{:S(2)}) collective-permute-start(bf16[4,384,128]{2,1,0:T(8,128)(2,1)S(1)} %bitcast.13), channel_id=1, source_target_pairs={{0,64},{64,128},{128,192},{192,256},{256,320},{320,384},{384,448},... | collective-permute-start | bytes 1179656 | tf_op jit(solution)/shard_map/ppermute | solution.py:35
  30.5 0.7 select_reduce_fusion.pages
  31.3 2.4 %attend_blocks.5 = (f32[1024,128]{1,0:T(8,128)S(1)}, f32[1024,256]{1,0:T(8,128)S(1)}) custom-call(s32[3]{0:T(128)S(1)} %pad_add_fusion.scal, bf16[128,1024]{1,0:T(8,128)(2,1)S(1)} %bitcast.16, bf16[4,384,128]{2,1,0:T(8,128)(2,1)S(1)} %bitcast.14), custom_call_target="tpu_custom_call" | custom-call | flops 4026531840 | bytes 393216 | tf_op jit(solution)/shard_map/attend_blocks/pallas_call | solution.py:129
  33.7 4.6 %collective-permute-start.4 = (bf16[4,384,128]{2,1,0:T(8,128)(2,1)S(1)}, bf16[4,384,128]{2,1,0:T(8,128)(2,1)S(1)}, u32[]{:S(2)}, u32[]{:S(2)}) collective-permute-start(bf16[4,384,128]{2,1,0:T(8,128)(2,1)S(1)} %collective-permute-done.3.refs_1_), channel_id=1, source_target_pairs={{0,448},{64,0},{128,64},{192,128},{256,192},{320,256},{384,320},{4... | collective-permute-start | bytes 1179656 | tf_op jit(solution)/shard_map/ppermute | solution.py:35
  38.3 1.9 %collective-permute-start.1 = (bf16[4,384,128]{2,1,0:T(8,128)(2,1)S(1)}, bf16[4,384,128]{2,1,0:T(8,128)(2,1)S(1)}, u32[]{:S(2)}, u32[]{:S(2)}) collective-permute-start(bf16[4,384,128]{2,1,0:T(8,128)(2,1)S(1)} %collective-permute-done.refs_0_.refs_7_), channel_id=1, source_target_pairs={{0,64},{64,128},{128,192},{192,256},{256,320},{320,384},{384,448},... | collective-permute-start | bytes 1179656 | tf_op jit(solution)/shard_map/ppermute | solution.py:35
  40.2 2.8 %attend_blocks.6 = (f32[1024,128]{1,0:T(8,128)S(1)}, f32[1024,256]{1,0:T(8,128)S(1)}) custom-call(s32[3]{0:T(128)S(1)} %pad_add_fusion.scal, bf16[128,1024]{1,0:T(8,128)(2,1)S(1)} %bitcast.17, bf16[4,384,128]{2,1,0:T(8,128)(2,1)S(1)} %collective-permute-done.refs_0_.refs_7_, ...), custom_call_target="tpu_custom_call", output_to_operand_aliasing={{0}: (4, {}), {1}: (5, {})} | custom-call | flops 8053063680 | bytes 786432 | tf_op jit(solution)/shard_map/attend_blocks/pallas_call | solution.py:129
  43.4 5.3 %collective-permute-start.5 = (bf16[4,384,128]{2,1,0:T(8,128)(2,1)S(1)}, bf16[4,384,128]{2,1,0:T(8,128)(2,1)S(1)}, u32[]{:S(2)}, u32[]{:S(2)}) collective-permute-start(bf16[4,384,128]{2,1,0:T(8,128)(2,1)S(1)} %collective-permute-done.4.refs_1_.refs_2_), channel_id=1, source_target_pairs={{0,448},{64,0},{128,64},{192,128},{256,192},{320,256},{384,320},{4... | collective-permute-start | bytes 1179656 | tf_op jit(solution)/shard_map/ppermute | solution.py:35
  48.7 1.9 %collective-permute-start.2 = (bf16[4,384,128]{2,1,0:T(8,128)(2,1)S(1)}, bf16[4,384,128]{2,1,0:T(8,128)(2,1)S(1)}, u32[]{:S(2)}, u32[]{:S(2)}) collective-permute-start(bf16[4,384,128]{2,1,0:T(8,128)(2,1)S(1)} %collective-permute-done.1.refs_0_.refs_6_), channel_id=1, source_target_pairs={{0,64},{64,128},{128,192},{192,256},{256,320},{320,384},{384,448},... | collective-permute-start | bytes 1179656 | tf_op jit(solution)/shard_map/ppermute | solution.py:35
  50.6 3.0 %attend_blocks.7 = (f32[1024,128]{1,0:T(8,128)S(1)}, f32[1024,256]{1,0:T(8,128)S(1)}) custom-call(s32[3]{0:T(128)S(1)} %pad_add_fusion.scal, bf16[128,1024]{1,0:T(8,128)(2,1)S(1)} %bitcast.18, bf16[4,384,128]{2,1,0:T(8,128)(2,1)S(1)} %collective-permute-done.1.refs_0_.refs_6_, ...), custom_call_target="tpu_custom_call", output_to_operand_aliasing={{0}: (4, {}), {1}: (5, {})} | custom-call | flops 8053063680 | bytes 786432 | tf_op jit(solution)/shard_map/attend_blocks/pallas_call | solution.py:129
  53.6 4.8 %collective-permute-done.2.refs_0_.refs_5_ = bf16[4,384,128]{2,1,0:T(8,128)(2,1)S(1)} collective-permute-done((bf16[4,384,128]{2,1,0:T(8,128)(2,1)S(1)}, bf16[4,384,128]{2,1,0:T(8,128)(2,1)S(1)}, u32[]{:S(2)}, u32[]{:S(2)}) %collective-permute-start.2) | collective-permute-done | bytes 393248 | tf_op jit(solution)/shard_map/ppermute | solution.py:35
  58.5 1.9 %collective-permute-start.6 = (bf16[4,384,128]{2,1,0:T(8,128)(2,1)S(1)}, bf16[4,384,128]{2,1,0:T(8,128)(2,1)S(1)}, u32[]{:S(2)}, u32[]{:S(2)}) collective-permute-start(bf16[4,384,128]{2,1,0:T(8,128)(2,1)S(1)} %broadcast_select_fusion), channel_id=1, source_target_pairs={{0,64},{1,449},{64,128},{65,1},{128,192},{129,65},{192,256},{193,1... | collective-permute-start | bytes 1179656 | tf_op jit(solution)/shard_map/ppermute | solution.py:229
  60.4 3.0 %attend_blocks.8 = (f32[1024,128]{1,0:T(8,128)S(1)}, f32[1024,256]{1,0:T(8,128)S(1)}) custom-call(s32[3]{0:T(128)S(1)} %pad_add_fusion.scal, bf16[128,1024]{1,0:T(8,128)(2,1)S(1)} %bitcast.19, bf16[4,384,128]{2,1,0:T(8,128)(2,1)S(1)} %collective-permute-done.2.refs_0_.refs_5_, ...), custom_call_target="tpu_custom_call", output_to_operand_aliasing={{0}: (4, {}), {1}: (5, {})} | custom-call | flops 8053063680 | bytes 786432 | tf_op jit(solution)/shard_map/attend_blocks/pallas_call | solution.py:129
  63.5 1.0 %copy-done.12 = f32[1024,256]{1,0:T(8,128)} copy-done((f32[1024,256]{1,0:T(8,128)}, f32[1024,256]{1,0:T(8,128)S(1)}, u32[]{:S(2)}) %copy-start.12) | copy-done | bytes 1048600
  64.5 2.5 %collective-permute-done.6.refs_0_.refs_4_ = bf16[4,384,128]{2,1,0:T(8,128)(2,1)S(1)} collective-permute-done((bf16[4,384,128]{2,1,0:T(8,128)(2,1)S(1)}, bf16[4,384,128]{2,1,0:T(8,128)(2,1)S(1)}, u32[]{:S(2)}, u32[]{:S(2)}) %collective-permute-start.6) | collective-permute-done | bytes 393248 | tf_op jit(solution)/shard_map/ppermute | solution.py:229
  67.0 0.8 copy-done.7
  67.8 2.5 %pick_pages.1 = bf16[8,2,32,128]{3,2,1,0:T(8,128)(2,1)} custom-call(s32[3]{0:T(128)} %copy-done.9, s32[8]{0:T(128)} %select_reduce_fusion.pages, bf16[4,384,128]{2,1,0:T(8,128)(2,1)} %bitcast.15, bf16[4,384,128]{2,1,0:T(8,128)(2,1)} %copy-done.3, bf16[4,384,128]{2,1,0:T(8,128)(2,1)} %copy-done.5, bf16[4,384,128]{2,1,0:T(8,128)(2,1)} %copy-done.1, ...), custom_call_target="tpu_custom_call" | custom-call | tf_op jit(solution)/shard_map/pick_pages/pallas_call | solution.py:191
  70.3 13.3 %all-to-all-start = ((bf16[16,32,128]{2,1,0:T(8,128)(2,1)}), bf16[16,32,128]{2,1,0:T(8,128)(2,1)S(1)}, u32[]{:S(2)}, u32[]{:S(2)}) async-start(bf16[16,32,128]{2,1,0:T(8,128)(2,1)} %bitcast.21), calls=%async_computation | async-start | bytes 262144 | tf_op jit(solution)/shard_map/all_to_all | solution.py:250
  84.2 1.0 %copy-done.8 = bf16[4,384,128]{2,1,0:T(8,128)(2,1)S(1)} copy-done((bf16[4,384,128]{2,1,0:T(8,128)(2,1)S(1)}, bf16[4,384,128]{2,1,0:T(8,128)(2,1)}, u32[]{:S(2)}) %copy-start.8) | copy-done | bytes 393240
  85.2 2.4 %attend_blocks.9 = bf16[128,1024]{1,0:T(8,128)(2,1)} custom-call(s32[3]{0:T(128)S(1)} %copy-done.10, bf16[128,1024]{1,0:T(8,128)(2,1)S(1)} %bitcast.20, bf16[4,384,128]{2,1,0:T(8,128)(2,1)S(1)} %copy-done.8, f32[1024,128]{1,0:T(8,128)S(1)} %get-tuple-element.19.refs_1_, f32[1024,256]{1,0:T(8,128)S(1)} %copy-done.13), custom_call_target="tpu_custom_call" | custom-call | flops 4026531840 | bytes 393216 | tf_op jit(solution)/shard_map/attend_blocks/pallas_call | solution.py:129
  87.6 2.0 %all-to-all-done = bf16[16,32,128]{2,1,0:T(8,128)(2,1)S(1)} async-done(((bf16[16,32,128]{2,1,0:T(8,128)(2,1)}), bf16[16,32,128]{2,1,0:T(8,128)(2,1)S(1)}, u32[]{:S(2)}, u32[]{:S(2)}) %all-to-all-start) | async-done | bytes 131104 | tf_op jit(solution)/shard_map/all_to_all | solution.py:250
  90.3 1.5 %assemble_pages.1 = (bf16[1,16,1024]{2,1,0:T(8,128)(2,1)}, bf16[1,16,1024]{2,1,0:T(8,128)(2,1)}) custom-call(s32[1]{0:T(128)} %bitcast.8.core, bf16[8,2,32,128]{3,2,1,0:T(8,128)(2,1)} %bitcast.22), custom_call_target="tpu_custom_call" | custom-call | tf_op jit(solution)/shard_map/assemble_pages/pallas_call | solution.py:214
  (37 shorter events, 2.5 us)
Async XLA Ops:
  1.4 29.8 %copy-start.11 = (bf16[1,128,1024]{2,1,0:T(8,128)(2,1)S(1)}, bf16[1,128,1024]{2,1,0:T(8,128)(2,1)}, u32[]{:S(2)}) copy-start(bf16[1,128,1024]{2,1,0:T(8,128)(2,1)} %param.8) | copy-start | bytes 786436
  21.5 12.2 %copy-start = (bf16[1536,128]{1,0:T(8,128)(2,1)}, bf16[1536,128]{1,0:T(8,128)(2,1)S(1)}, u32[]{:S(2)}) copy-start(bf16[1536,128]{1,0:T(8,128)(2,1)S(1)} %all-gather) | copy-start | bytes 1179652
  21.5 12.2 %collective-permute-start.3 = (bf16[4,384,128]{2,1,0:T(8,128)(2,1)S(1)}, bf16[4,384,128]{2,1,0:T(8,128)(2,1)S(1)}, u32[]{:S(2)}, u32[]{:S(2)}) collective-permute-start(bf16[4,384,128]{2,1,0:T(8,128)(2,1)S(1)} %bitcast.12), channel_id=1, source_target_pairs={{0,448},{64,0},{128,64},{192,128},{256,192},{320,256},{384,320},{4... | collective-permute-start | bytes 1179656 | tf_op jit(solution)/shard_map/ppermute | solution.py:35
  26.6 11.7 %collective-permute-start = (bf16[4,384,128]{2,1,0:T(8,128)(2,1)S(1)}, bf16[4,384,128]{2,1,0:T(8,128)(2,1)S(1)}, u32[]{:S(2)}, u32[]{:S(2)}) collective-permute-start(bf16[4,384,128]{2,1,0:T(8,128)(2,1)S(1)} %bitcast.13), channel_id=1, source_target_pairs={{0,64},{64,128},{128,192},{192,256},{256,320},{320,384},{384,448},... | collective-permute-start | bytes 1179656 | tf_op jit(solution)/shard_map/ppermute | solution.py:35
  29.8 0.7 copy-start.15
  31.3 29.2 %copy-start.9 = (s32[3]{0:T(128)}, s32[3]{0:T(128)S(1)}, u32[]{:S(2)}) copy-start(s32[3]{0:T(128)S(1)} %pad_add_fusion.scal) | copy-start | bytes 40
  33.6 9.3 %copy-start.3 = (bf16[4,384,128]{2,1,0:T(8,128)(2,1)}, bf16[4,384,128]{2,1,0:T(8,128)(2,1)S(1)}, u32[]{:S(2)}) copy-start(bf16[4,384,128]{2,1,0:T(8,128)(2,1)S(1)} %collective-permute-done.3.refs_1_) | copy-start | bytes 1179652
  33.7 9.7 %collective-permute-start.4 = (bf16[4,384,128]{2,1,0:T(8,128)(2,1)S(1)}, bf16[4,384,128]{2,1,0:T(8,128)(2,1)S(1)}, u32[]{:S(2)}, u32[]{:S(2)}) collective-permute-start(bf16[4,384,128]{2,1,0:T(8,128)(2,1)S(1)} %collective-permute-done.3.refs_1_), channel_id=1, source_target_pairs={{0,448},{64,0},{128,64},{192,128},{256,192},{320,256},{384,320},{4... | collective-permute-start | bytes 1179656 | tf_op jit(solution)/shard_map/ppermute | solution.py:35
  38.2 4.7 %copy-start.4 = (bf16[4,384,128]{2,1,0:T(8,128)(2,1)}, bf16[4,384,128]{2,1,0:T(8,128)(2,1)S(1)}, u32[]{:S(2)}) copy-start(bf16[4,384,128]{2,1,0:T(8,128)(2,1)S(1)} %collective-permute-done.refs_0_.refs_7_) | copy-start | bytes 1179652
  38.3 10.4 %collective-permute-start.1 = (bf16[4,384,128]{2,1,0:T(8,128)(2,1)S(1)}, bf16[4,384,128]{2,1,0:T(8,128)(2,1)S(1)}, u32[]{:S(2)}, u32[]{:S(2)}) collective-permute-start(bf16[4,384,128]{2,1,0:T(8,128)(2,1)S(1)} %collective-permute-done.refs_0_.refs_7_), channel_id=1, source_target_pairs={{0,64},{64,128},{128,192},{192,256},{256,320},{320,384},{384,448},... | collective-permute-start | bytes 1179656 | tf_op jit(solution)/shard_map/ppermute | solution.py:35
  43.4 10.2 %copy-start.5 = (bf16[4,384,128]{2,1,0:T(8,128)(2,1)}, bf16[4,384,128]{2,1,0:T(8,128)(2,1)S(1)}, u32[]{:S(2)}) copy-start(bf16[4,384,128]{2,1,0:T(8,128)(2,1)S(1)} %collective-permute-done.4.refs_1_.refs_2_) | copy-start | bytes 1179652
  43.4 10.2 %collective-permute-start.5 = (bf16[4,384,128]{2,1,0:T(8,128)(2,1)S(1)}, bf16[4,384,128]{2,1,0:T(8,128)(2,1)S(1)}, u32[]{:S(2)}, u32[]{:S(2)}) collective-permute-start(bf16[4,384,128]{2,1,0:T(8,128)(2,1)S(1)} %collective-permute-done.4.refs_1_.refs_2_), channel_id=1, source_target_pairs={{0,448},{64,0},{128,64},{192,128},{256,192},{320,256},{384,320},{4... | collective-permute-start | bytes 1179656 | tf_op jit(solution)/shard_map/ppermute | solution.py:35
  48.7 4.9 %copy-start.6 = (bf16[4,384,128]{2,1,0:T(8,128)(2,1)}, bf16[4,384,128]{2,1,0:T(8,128)(2,1)S(1)}, u32[]{:S(2)}) copy-start(bf16[4,384,128]{2,1,0:T(8,128)(2,1)S(1)} %collective-permute-done.1.refs_0_.refs_6_) | copy-start | bytes 1179652
  48.7 9.7 %collective-permute-start.2 = (bf16[4,384,128]{2,1,0:T(8,128)(2,1)S(1)}, bf16[4,384,128]{2,1,0:T(8,128)(2,1)S(1)}, u32[]{:S(2)}, u32[]{:S(2)}) collective-permute-start(bf16[4,384,128]{2,1,0:T(8,128)(2,1)S(1)} %collective-permute-done.1.refs_0_.refs_6_), channel_id=1, source_target_pairs={{0,64},{64,128},{128,192},{192,256},{256,320},{320,384},{384,448},... | collective-permute-start | bytes 1179656 | tf_op jit(solution)/shard_map/ppermute | solution.py:35
  53.6 6.8 %copy-start.1 = (bf16[4,384,128]{2,1,0:T(8,128)(2,1)}, bf16[4,384,128]{2,1,0:T(8,128)(2,1)S(1)}, u32[]{:S(2)}) copy-start(bf16[4,384,128]{2,1,0:T(8,128)(2,1)S(1)} %collective-permute-done.5.refs_1_.refs_3_) | copy-start | bytes 1179652
  58.4 2.0 %copy-start.2 = (bf16[4,384,128]{2,1,0:T(8,128)(2,1)}, bf16[4,384,128]{2,1,0:T(8,128)(2,1)S(1)}, u32[]{:S(2)}) copy-start(bf16[4,384,128]{2,1,0:T(8,128)(2,1)S(1)} %collective-permute-done.2.refs_0_.refs_5_) | copy-start | bytes 1179652
  58.5 8.5 %collective-permute-start.6 = (bf16[4,384,128]{2,1,0:T(8,128)(2,1)S(1)}, bf16[4,384,128]{2,1,0:T(8,128)(2,1)S(1)}, u32[]{:S(2)}, u32[]{:S(2)}) collective-permute-start(bf16[4,384,128]{2,1,0:T(8,128)(2,1)S(1)} %broadcast_select_fusion), channel_id=1, source_target_pairs={{0,64},{1,449},{64,128},{65,1},{128,192},{129,65},{192,256},{193,1... | collective-permute-start | bytes 1179656 | tf_op jit(solution)/shard_map/ppermute | solution.py:229
  63.4 1.0 %copy-start.12 = (f32[1024,256]{1,0:T(8,128)}, f32[1024,256]{1,0:T(8,128)S(1)}, u32[]{:S(2)}) copy-start(f32[1024,256]{1,0:T(8,128)S(1)} %get-tuple-element.20.refs_2_) | copy-start | bytes 3145732
  67.0 0.8 copy-start.7
  67.8 15.8 %copy-start.13 = (f32[1024,256]{1,0:T(8,128)S(1)}, f32[1024,256]{1,0:T(8,128)}, u32[]{:S(2)}) copy-start(f32[1024,256]{1,0:T(8,128)} %copy-done.12) | copy-start | bytes 3145732
  70.3 19.4 %all-to-all-start = ((bf16[16,32,128]{2,1,0:T(8,128)(2,1)}), bf16[16,32,128]{2,1,0:T(8,128)(2,1)S(1)}, u32[]{:S(2)}, u32[]{:S(2)}) async-start(bf16[16,32,128]{2,1,0:T(8,128)(2,1)} %bitcast.21), calls=%async_computation | async-start | bytes 262144 | tf_op jit(solution)/shard_map/all_to_all | solution.py:250
  83.5 0.7 copy-start.10
  84.2 1.0 %copy-start.8 = (bf16[4,384,128]{2,1,0:T(8,128)(2,1)S(1)}, bf16[4,384,128]{2,1,0:T(8,128)(2,1)}, u32[]{:S(2)}) copy-start(bf16[4,384,128]{2,1,0:T(8,128)(2,1)} %copy-done.7) | copy-start | bytes 1179652
  89.7 0.6 copy-start.14

commit v3 on v2

--- a/solution.py
+++ b/solution.py
@@ -40,17 +40,10 @@
     blocks, refs = refs[:count], refs[count:]
     if not first:
         m_ref, acc_ref, *refs = refs
-    o_ref = None
     if last:
-        o_ref, *refs = refs
-    elif first:
-        m_ref, acc_ref, *refs = refs
+        (o_ref,) = refs
     else:
-        m_ref, acc_ref, *refs = refs
-    held, arrived = refs
-    copies = [pltpu.make_async_copy(blocks[i], held.at[i], arrived.at[i]) for i in range(count)]
-    for copy in copies:
-        copy.start()
+        m_ref, acc_ref = refs
     if first:
         m_ref[...] = jnp.full(m_ref.shape, -1e30, jnp.float32)
         acc_ref[...] = jnp.zeros(acc_ref.shape, jnp.float32)
@@ -63,10 +56,10 @@
     def step(i, j, masked, with_new=True):
         new_keys = STEP_NEW if with_new else 0
         width = new_keys + STEP_OLD
-        k = [held[i, z, 0:NEW, :] for z in range(Z)] if with_new else []
-        k += [held[i, z, 2 * NEW : 2 * NEW + OLD, :] for z in range(Z)]
-        v = [held[i, z, NEW : 2 * NEW, :] for z in range(Z)] if with_new else []
-        v += [held[i, z, 2 * NEW + OLD : ROWS, :] for z in range(Z)]
+        k = [blocks[i][z, 0:NEW, :] for z in range(Z)] if with_new else []
+        k += [blocks[i][z, 2 * NEW : 2 * NEW + OLD, :] for z in range(Z)]
+        v = [blocks[i][z, NEW : 2 * NEW, :] for z in range(Z)] if with_new else []
+        v += [blocks[i][z, 2 * NEW + OLD : ROWS, :] for z in range(Z)]
         k, v = jnp.concatenate(k, axis=0), jnp.concatenate(v, axis=0)
         v = jnp.concatenate([v, jnp.ones_like(v)], axis=1)
 
@@ -99,7 +92,6 @@
             s = ahead
 
     for i, far in enumerate(apart):
-        copies[i].wait()
         j = lax.rem(y + far + Y, Y)
         old_full = (j + 1) * STEP_OLD <= prefix
         old_some = j * STEP_OLD < prefix
@@ -129,16 +121,12 @@
     return pl.pallas_call(
         functools.partial(attend_kernel, apart=apart, first=first, last=last),
         in_specs=[pl.BlockSpec(memory_space=pltpu.SMEM), whole]
-        + [pl.BlockSpec(memory_space=pl.ANY)] * count
+        + [whole] * count
         + ([] if first else [whole] * 2),
         out_specs=whole if last else (whole, whole),
         out_shape=jax.ShapeDtypeStruct((NEW, HEADS * HEAD), jnp.bfloat16) if last else saved,
         input_output_aliases={} if first or last else {2 + count: 0, 3 + count: 1},
-        scratch_shapes=[
-            pltpu.VMEM((count, Z, ROWS, HEAD), jnp.bfloat16),
-            pltpu.SemaphoreType.DMA((count,)),
-        ],
-        compiler_params=pltpu.CompilerParams(vmem_limit_bytes=32 << 20),
+        compiler_params=pltpu.CompilerParams(vmem_limit_bytes=24 << 20),
         cost_estimate=pl.CostEstimate(
             flops=COST * HEADS * NEW * keys * HEAD,
             bytes_accessed=count * Z * ROWS * HEAD * 2,
@@ -152,51 +140,36 @@
 
 
 def pick_kernel(scal, pages, *refs):
-    blocks, (o_ref, held, arrived) = refs[:Y], refs[Y:]
+    blocks, o_ref = refs[:Y], refs[Y]
     y, length = lax.div(scal[0], Z), scal[1]
-    count = held.shape[0]
-    for k in range(count):
+    row = lax.broadcasted_iota(jnp.int32, (PAGE, HEAD), 0)
+    for k in range(o_ref.shape[0]):
         page = pages[k]
         away = lax.rem(lax.div(page, PAGES) - y + Y, Y)
         inside = lax.rem(page, PAGES)
         z = lax.div(inside, NEW // PAGE)
         first = pl.multiple_of(lax.rem(inside, NEW // PAGE) * PAGE, PAGE)
+        keep = row < length - page * PAGE
         for d in range(Y):
 
             @pl.when(away == d)
             def _():
                 for half in range(2):
-                    pltpu.make_async_copy(
-                        blocks[d].at[z, pl.ds(half * NEW + first, PAGE)],
-                        held.at[k, pl.ds(half * PAGE, PAGE)],
-                        arrived.at[k, half],
-                    ).start()
-
-    row = lax.broadcasted_iota(jnp.int32, (PAGE, HEAD), 0)
-    for k in range(count):
-        keep = row < length - pages[k] * PAGE
-        for half in range(2):
-            rows = pl.ds(half * PAGE, PAGE)
-            pltpu.make_async_copy(
-                blocks[0].at[0, pl.ds(0, PAGE)], held.at[k, rows], arrived.at[k, half]
-            ).wait()
-            page = jnp.where(keep, held[k, rows, :].astype(jnp.float32), 0.0).astype(jnp.bfloat16)
-            for core in range(2):
-                o_ref[k, core, rows, :] = page
+                    rows = blocks[d][z, pl.ds(half * NEW + first, PAGE), :]
+                    rows = jnp.where(keep, rows.astype(jnp.float32), 0.0).astype(jnp.bfloat16)
+                    for core in range(2):
+                        o_ref[k, core, half * PAGE : (half + 1) * PAGE, :] = rows
 
 
 def pick(scal, pages, blocks):
     count = pages.shape[0]
-    small = pl.BlockSpec(memory_space=pltpu.SMEM)
+    small, whole = pl.BlockSpec(memory_space=pltpu.SMEM), pl.BlockSpec(memory_space=pltpu.VMEM)
     return pl.pallas_call(
         pick_kernel,
-        in_specs=[small, small] + [pl.BlockSpec(memory_space=pl.ANY)] * Y,
-        out_specs=pl.BlockSpec(memory_space=pltpu.VMEM),
+        in_specs=[small, small] + [whole] * Y,
+        out_specs=whole,
         out_shape=jax.ShapeDtypeStruct((count, 2, 2 * PAGE, HEAD), jnp.bfloat16),
-        scratch_shapes=[
-            pltpu.VMEM((count, 2 * PAGE, HEAD), jnp.bfloat16),
-            pltpu.SemaphoreType.DMA((count, 2)),
-        ],
+        compiler_params=pltpu.CompilerParams(vmem_limit_bytes=8 << 20),
         name="pick_pages",
     )(scal, pages, *blocks)
 
@@ -216,17 +189,9 @@
         in_specs=[pl.BlockSpec(memory_space=pltpu.SMEM), whole],
         out_specs=(whole, whole),
         out_shape=(jax.ShapeDtypeStruct((1, PAGE, tps * HEAD), jnp.bfloat16),) * 2,
+        compiler_params=pltpu.CompilerParams(vmem_limit_bytes=8 << 20),
         name="assemble_pages",
     )(core, got)
-
-
-def farthest(right, left):
-    core = lax.axis_index("core")
-    pairs = []
-    for i in range(2 * Y):
-        y, c = i // 2, i % 2
-        pairs.append((i, (y + (1 if c == 0 else -1)) % Y * 2 + c))
-    return lax.ppermute(jnp.where(core == 0, right, left), ("y", "core"), pairs)
 
 
 def body(q, new_k, new_v, old_k, old_v, prompt_len, prefix_len, slots):
@@ -236,23 +201,23 @@
     scal = jnp.stack([ctx, prompt_len[0], prefix_len[0]])
     mine = jnp.concatenate([new_k[0], new_v[0], old_k[0], old_v[0]], axis=0)
     column = lax.all_gather(mine, "zh", axis=0)
-    right, left = [column], [column]
+    a, b = [column], [column]
     for _ in range(3):
-        right.append(shift(right[-1], ("y",), (1,), (Y,)))
-        left.append(shift(left[-1], ("y",), (-1,), (Y,)))
-    far = farthest(right[3], left[3])
+        a.append(shift(a[-1], ("y",), (1,), (Y,)))
+        b.append(shift(b[-1], ("y",), (-1,), (Y,)))
+    far = shift(a[3], ("y",), (1,), (Y,))
 
     slots_here = ctx * tps + jnp.arange(tps, dtype=jnp.int32)
     page_ids = jnp.arange(slots.shape[1], dtype=jnp.int32)
     pages = jnp.sum(jnp.where(slots[0][None, :] == slots_here[:, None], page_ids[None, :], 0), axis=1)
-    by_distance = [column, left[1], left[2], left[3], far, right[3], right[2], right[1]]
+    by_distance = [column, b[1], b[2], b[3], far, a[3], a[2], a[1]]
     sent = pick(scal, pages, by_distance).reshape(2 * tps, 2 * PAGE, HEAD)
     got = lax.all_to_all(sent, ("x", "zl", "core"), split_axis=0, concat_axis=0, tiled=True)
     pools = assemble(core[None], got.reshape(tps, 2, 2 * PAGE, HEAD))
 
     state = attend(scal, q[0], [column], (0,))
     for away in (1, 2, 3):
-        state = attend(scal, q[0], [right[away], left[away]], (-away, away), state)
+        state = attend(scal, q[0], [a[away], b[away]], (-away, away), state)
     out = attend(scal, q[0], [far], (4,), state, last=True)
     return (out[None], *pools)
 

time: 92.5 us -> 84.2 us (0.910)
  Pallas kernels: 17.6 us -> 8.92 us
  waiting for transfers between devices: 9.77 us -> 16.9 us
  local copies, waits for them, and re-layouts: 4.76 us -> 0.68 us
  starting transfers between devices: 35.9 us -> 34 us
    ppermute x6 -> x7, waiting for transfers between devices: 5.19 us -> 12.1 us  [shift(): return lax.ppermute(value, axes, [(i, moved(i)) for i in range(count)])]
    pallas_call x5, Pallas kernels: 13.5 us -> 6.64 us  [attend(): pl.pallas_call(functools.partial(attend_kernel, apart=apart, first=first,...]
    unnamed x32 -> x4, local copies, waits for them, and re-layouts: 4.76 us -> 0.68 us
    all_to_all x1, waiting for transfers between devices: 2.04 us -> 4.79 us  [body(): lax.all_to_all(sent, ('x', 'zl', 'core'), split_axis=0, concat_axis=0, ti...]
    ppermute x1 -> x0, waiting for transfers between devices: 2.54 us -> none  [farthest(): return lax.ppermute(jnp.where(core == 0, right, left), ('y', 'core'), pairs)]
    ppermute x1 -> x0, starting transfers between devices: 1.92 us -> none  [farthest(): return lax.ppermute(jnp.where(core == 0, right, left), ('y', 'core'), pairs)]
    ppermute x6 -> x7, starting transfers between devices: 20.7 us -> 21.9 us  [shift(): return lax.ppermute(value, axes, [(i, moved(i)) for i in range(count)])]
    all_to_all x1, starting transfers between devices: 13.3 us -> 12.2 us  [body(): lax.all_to_all(sent, ('x', 'zl', 'core'), split_axis=0, concat_axis=0, ti...]
  transfers between devices with their start and end apart: 8 -> 8, of which waited for: 4 -> 5; matrix products, arithmetic and copies ran while one was open for 1% -> 0% of each run, Pallas kernels for 15% -> 8%
where the time goes in v3:
time: 84.2 us; the launch traced here: 83.7 us
  starting transfers between devices  34 us (40%)
  blocking collectives  20 us (24%)
  waiting for transfers between devices  16.9 us (20%)
  Pallas kernels  8.92 us (11%)
  between operations  2.07 us (2%)
  other arithmetic  1.08 us (1%)
    ppermute x7, starting transfers between devices, shift(): return lax.ppermute(value, axes, [(i, moved(i)) for i in range(count)])  21.9 us
    all_gather x1, blocking collectives, body(): column = lax.all_gather(mine, 'zh', axis=0)  20 us
    all_to_all x1, starting transfers between devices, body(): lax.all_to_all(sent, ('x', 'zl', 'core'), split_axis=0, concat_axis=0, ti...  12.2 us
    ppermute x7, waiting for transfers between devices, shift(): return lax.ppermute(value, axes, [(i, moved(i)) for i in range(count)])  12.1 us
    pallas_call x5, Pallas kernels, attend(): pl.pallas_call(functools.partial(attend_kernel, apart=apart, first=first,...  6.64 us
    all_to_all x1, waiting for transfers between devices, body(): lax.all_to_all(sent, ('x', 'zl', 'core'), split_axis=0, concat_axis=0, ti...  4.79 us
  transfers between devices with their start and end apart: 8, of which 5 were waited for; matrix products, arithmetic and copies ran while one was open for 0% of the time, Pallas kernels for 8%

profile of v3, /device:TPU:1, one launch (start us, length us, event | category | flops | bytes accessed | tf_op | source)
XLA Modules:
  0.0 83.7 jit_solution(13257483080575326569)
XLA Ops:
  0.6 0.8 pad_maximum_fusion
  1.5 20.0 %all-gather = bf16[1536,128]{1,0:T(8,128)(2,1)S(1)} all-gather(bf16[384,128]{1,0:T(8,128)(2,1)S(1)} %pad_maximum_fusion), channel_id=2, replica_groups=mesh['y'=8,'zh'=4,'x'=4,'zl'=2,'core'=2] {'zh'}, dimensions={0}, use_global_device_ids=true | all-gather | bytes 491520 | tf_op jit(solution)/shard_map/all_gather | solution.py:203
  21.5 3.2 %collective-permute-start = (bf16[4,384,128]{2,1,0:T(8,128)(2,1)S(1)}, bf16[4,384,128]{2,1,0:T(8,128)(2,1)S(1)}, u32[]{:S(2)}, u32[]{:S(2)}) collective-permute-start(bf16[4,384,128]{2,1,0:T(8,128)(2,1)S(1)} %bitcast.12), channel_id=1, source_target_pairs={{0,64},{64,128},{128,192},{192,256},{256,320},{320,384},{384,448},... | collective-permute-start | bytes 1179656 | tf_op jit(solution)/shard_map/ppermute | solution.py:35
  24.7 3.8 %collective-permute-start.4 = (bf16[4,384,128]{2,1,0:T(8,128)(2,1)S(1)}, bf16[4,384,128]{2,1,0:T(8,128)(2,1)S(1)}, u32[]{:S(2)}, u32[]{:S(2)}) collective-permute-start(bf16[4,384,128]{2,1,0:T(8,128)(2,1)S(1)} %bitcast.13), channel_id=1, source_target_pairs={{0,448},{64,0},{128,64},{192,128},{256,192},{320,256},{384,320},{4... | collective-permute-start | bytes 1179656 | tf_op jit(solution)/shard_map/ppermute | solution.py:35
  29.8 0.7 copy-done.1
  30.5 0.2 select_reduce_fusion.pages
  30.8 2.2 %attend_blocks.5 = (f32[1024,128]{1,0:T(8,128)S(1)}, f32[1024,256]{1,0:T(8,128)S(1)}) custom-call(s32[3]{0:T(128)S(1)} %pad_add_fusion.scal, bf16[128,1024]{1,0:T(8,128)(2,1)S(1)} %bitcast.17, bf16[4,384,128]{2,1,0:T(8,128)(2,1)S(1)} %bitcast.14), custom_call_target="tpu_custom_call" | custom-call | flops 4026531840 | bytes 393216 | tf_op jit(solution)/shard_map/attend_blocks/pallas_call | solution.py:121
  33.0 0.3 collective-permute-done.refs_0_.refs_7_
  33.3 1.9 %collective-permute-start.1 = (bf16[4,384,128]{2,1,0:T(8,128)(2,1)S(1)}, bf16[4,384,128]{2,1,0:T(8,128)(2,1)S(1)}, u32[]{:S(2)}, u32[]{:S(2)}) collective-permute-start(bf16[4,384,128]{2,1,0:T(8,128)(2,1)S(1)} %collective-permute-done.refs_0_.refs_7_), channel_id=1, source_target_pairs={{0,64},{64,128},{128,192},{192,256},{256,320},{320,384},{384,448},... | collective-permute-start | bytes 1179656 | tf_op jit(solution)/shard_map/ppermute | solution.py:35
  35.2 4.6 %collective-permute-start.5 = (bf16[4,384,128]{2,1,0:T(8,128)(2,1)S(1)}, bf16[4,384,128]{2,1,0:T(8,128)(2,1)S(1)}, u32[]{:S(2)}, u32[]{:S(2)}) collective-permute-start(bf16[4,384,128]{2,1,0:T(8,128)(2,1)S(1)} %collective-permute-done.4.refs_1_), channel_id=1, source_target_pairs={{0,448},{64,0},{128,64},{192,128},{256,192},{320,256},{384,320},{4... | collective-permute-start | bytes 1179656 | tf_op jit(solution)/shard_map/ppermute | solution.py:35
  39.8 1.5 %attend_blocks.6 = (f32[1024,128]{1,0:T(8,128)S(1)}, f32[1024,256]{1,0:T(8,128)S(1)}) custom-call(s32[3]{0:T(128)S(1)} %pad_add_fusion.scal, bf16[128,1024]{1,0:T(8,128)(2,1)S(1)} %bitcast.18, bf16[4,384,128]{2,1,0:T(8,128)(2,1)S(1)} %collective-permute-done.refs_0_.refs_7_, ...), custom_call_target="tpu_custom_call", output_to_operand_aliasing={{0}: (4, {}), {1}: (5, {})} | custom-call | flops 8053063680 | bytes 786432 | tf_op jit(solution)/shard_map/attend_blocks/pallas_call | solution.py:121
  41.3 2.3 %collective-permute-done.1.refs_0_.refs_6_ = bf16[4,384,128]{2,1,0:T(8,128)(2,1)S(1)} collective-permute-done((bf16[4,384,128]{2,1,0:T(8,128)(2,1)S(1)}, bf16[4,384,128]{2,1,0:T(8,128)(2,1)S(1)}, u32[]{:S(2)}, u32[]{:S(2)}) %collective-permute-start.1) | collective-permute-done | bytes 393248 | tf_op jit(solution)/shard_map/ppermute | solution.py:35
  43.7 1.9 %collective-permute-start.2 = (bf16[4,384,128]{2,1,0:T(8,128)(2,1)S(1)}, bf16[4,384,128]{2,1,0:T(8,128)(2,1)S(1)}, u32[]{:S(2)}, u32[]{:S(2)}) collective-permute-start(bf16[4,384,128]{2,1,0:T(8,128)(2,1)S(1)} %collective-permute-done.1.refs_0_.refs_6_), channel_id=1, source_target_pairs={{0,64},{64,128},{128,192},{192,256},{256,320},{320,384},{384,448},... | collective-permute-start | bytes 1179656 | tf_op jit(solution)/shard_map/ppermute | solution.py:35
  45.6 4.6 %collective-permute-start.6 = (bf16[4,384,128]{2,1,0:T(8,128)(2,1)S(1)}, bf16[4,384,128]{2,1,0:T(8,128)(2,1)S(1)}, u32[]{:S(2)}, u32[]{:S(2)}) collective-permute-start(bf16[4,384,128]{2,1,0:T(8,128)(2,1)S(1)} %collective-permute-done.5.refs_1_.refs_2_), channel_id=1, source_target_pairs={{0,448},{64,0},{128,64},{192,128},{256,192},{320,256},{384,320},{4... | collective-permute-start | bytes 1179656 | tf_op jit(solution)/shard_map/ppermute | solution.py:35
  50.2 0.8 attend_blocks.7
  50.9 2.4 %collective-permute-done.2.refs_0_.refs_5_ = bf16[4,384,128]{2,1,0:T(8,128)(2,1)S(1)} collective-permute-done((bf16[4,384,128]{2,1,0:T(8,128)(2,1)S(1)}, bf16[4,384,128]{2,1,0:T(8,128)(2,1)S(1)}, u32[]{:S(2)}, u32[]{:S(2)}) %collective-permute-start.2) | collective-permute-done | bytes 393248 | tf_op jit(solution)/shard_map/ppermute | solution.py:35
  53.4 1.9 %collective-permute-start.3 = (bf16[4,384,128]{2,1,0:T(8,128)(2,1)S(1)}, bf16[4,384,128]{2,1,0:T(8,128)(2,1)S(1)}, u32[]{:S(2)}, u32[]{:S(2)}) collective-permute-start(bf16[4,384,128]{2,1,0:T(8,128)(2,1)S(1)} %collective-permute-done.2.refs_0_.refs_5_), channel_id=1, source_target_pairs={{0,64},{64,128},{128,192},{192,256},{256,320},{320,384},{384,448},... | collective-permute-start | bytes 1179656 | tf_op jit(solution)/shard_map/ppermute | solution.py:35
  55.3 0.8 attend_blocks.8
  56.1 7.0 %collective-permute-done.3.refs_0_.refs_4_ = bf16[4,384,128]{2,1,0:T(8,128)(2,1)S(1)} collective-permute-done((bf16[4,384,128]{2,1,0:T(8,128)(2,1)S(1)}, bf16[4,384,128]{2,1,0:T(8,128)(2,1)S(1)}, u32[]{:S(2)}, u32[]{:S(2)}) %collective-permute-start.3) | collective-permute-done | bytes 393248 | tf_op jit(solution)/shard_map/ppermute | solution.py:35
  63.1 1.6 %pick_pages.1 = bf16[8,2,32,128]{3,2,1,0:T(8,128)(2,1)} custom-call(s32[3]{0:T(128)S(1)} %pad_add_fusion.scal, s32[8]{0:T(128)S(1)} %select_reduce_fusion.pages, bf16[4,384,128]{2,1,0:T(8,128)(2,1)S(1)} %bitcast.15, bf16[4,384,128]{2,1,0:T(8,128)(2,1)S(1)} %collective-permute-done.4.refs_1_, bf16[4,384,128]{2,1,0:T(8,128)(2,1)S(1)} %collective-permute-done.5.refs_1_.refs_2_, ...), custom_call_target="tpu_custom_call" | custom-call | tf_op jit(solution)/shard_map/pick_pages/pallas_call | solution.py:167
  64.7 12.2 %all-to-all-start = ((bf16[16,32,128]{2,1,0:T(8,128)(2,1)}), bf16[16,32,128]{2,1,0:T(8,128)(2,1)S(1)}, u32[]{:S(2)}, u32[]{:S(2)}) async-start(bf16[16,32,128]{2,1,0:T(8,128)(2,1)} %bitcast.10), calls=%async_computation | async-start | bytes 262144 | tf_op jit(solution)/shard_map/all_to_all | solution.py:215
  76.9 1.4 %attend_blocks.9 = bf16[128,1024]{1,0:T(8,128)(2,1)} custom-call(s32[3]{0:T(128)S(1)} %pad_add_fusion.scal, bf16[128,1024]{1,0:T(8,128)(2,1)S(1)} %bitcast.21, bf16[4,384,128]{2,1,0:T(8,128)(2,1)S(1)} %collective-permute-done.3.refs_0_.refs_4_, f32[1024,128]{1,0:T(8,128)S(1)} %get-tuple-element.19.refs_1_, f32[1024,256]{1,0:T(8,128)S(1)} %get-tuple-element.20.refs_2_), custom_call_target="tpu_custom_call" | custom-call | flops 4026531840 | bytes 393216 | tf_op jit(solution)/shard_map/attend_blocks/pallas_call | solution.py:121
  78.2 4.8 %all-to-all-done = bf16[16,32,128]{2,1,0:T(8,128)(2,1)S(1)} async-done(((bf16[16,32,128]{2,1,0:T(8,128)(2,1)}), bf16[16,32,128]{2,1,0:T(8,128)(2,1)S(1)}, u32[]{:S(2)}, u32[]{:S(2)}) %all-to-all-start) | async-done | bytes 131104 | tf_op jit(solution)/shard_map/all_to_all | solution.py:215
  83.0 0.6 assemble_pages.1
  (8 shorter events, 0.1 us)
Async XLA Ops:
  1.4 29.3 %copy-start = (bf16[1,128,1024]{2,1,0:T(8,128)(2,1)S(1)}, bf16[1,128,1024]{2,1,0:T(8,128)(2,1)}, u32[]{:S(2)}) copy-start(bf16[1,128,1024]{2,1,0:T(8,128)(2,1)} %param.8) | copy-start | bytes 786436
  21.5 11.8 %collective-permute-start = (bf16[4,384,128]{2,1,0:T(8,128)(2,1)S(1)}, bf16[4,384,128]{2,1,0:T(8,128)(2,1)S(1)}, u32[]{:S(2)}, u32[]{:S(2)}) collective-permute-start(bf16[4,384,128]{2,1,0:T(8,128)(2,1)S(1)} %bitcast.12), channel_id=1, source_target_pairs={{0,64},{64,128},{128,192},{192,256},{256,320},{320,384},{384,448},... | collective-permute-start | bytes 1179656 | tf_op jit(solution)/shard_map/ppermute | solution.py:35
  24.7 10.5 %collective-permute-start.4 = (bf16[4,384,128]{2,1,0:T(8,128)(2,1)S(1)}, bf16[4,384,128]{2,1,0:T(8,128)(2,1)S(1)}, u32[]{:S(2)}, u32[]{:S(2)}) collective-permute-start(bf16[4,384,128]{2,1,0:T(8,128)(2,1)S(1)} %bitcast.13), channel_id=1, source_target_pairs={{0,448},{64,0},{128,64},{192,128},{256,192},{320,256},{384,320},{4... | collective-permute-start | bytes 1179656 | tf_op jit(solution)/shard_map/ppermute | solution.py:35
  29.8 0.7 copy-start.1
  33.3 10.4 %collective-permute-start.1 = (bf16[4,384,128]{2,1,0:T(8,128)(2,1)S(1)}, bf16[4,384,128]{2,1,0:T(8,128)(2,1)S(1)}, u32[]{:S(2)}, u32[]{:S(2)}) collective-permute-start(bf16[4,384,128]{2,1,0:T(8,128)(2,1)S(1)} %collective-permute-done.refs_0_.refs_7_), channel_id=1, source_target_pairs={{0,64},{64,128},{128,192},{192,256},{256,320},{320,384},{384,448},... | collective-permute-start | bytes 1179656 | tf_op jit(solution)/shard_map/ppermute | solution.py:35
  35.2 10.4 %collective-permute-start.5 = (bf16[4,384,128]{2,1,0:T(8,128)(2,1)S(1)}, bf16[4,384,128]{2,1,0:T(8,128)(2,1)S(1)}, u32[]{:S(2)}, u32[]{:S(2)}) collective-permute-start(bf16[4,384,128]{2,1,0:T(8,128)(2,1)S(1)} %collective-permute-done.4.refs_1_), channel_id=1, source_target_pairs={{0,448},{64,0},{128,64},{192,128},{256,192},{320,256},{384,320},{4... | collective-permute-start | bytes 1179656 | tf_op jit(solution)/shard_map/ppermute | solution.py:35
  43.7 9.7 %collective-permute-start.2 = (bf16[4,384,128]{2,1,0:T(8,128)(2,1)S(1)}, bf16[4,384,128]{2,1,0:T(8,128)(2,1)S(1)}, u32[]{:S(2)}, u32[]{:S(2)}) collective-permute-start(bf16[4,384,128]{2,1,0:T(8,128)(2,1)S(1)} %collective-permute-done.1.refs_0_.refs_6_), channel_id=1, source_target_pairs={{0,64},{64,128},{128,192},{192,256},{256,320},{320,384},{384,448},... | collective-permute-start | bytes 1179656 | tf_op jit(solution)/shard_map/ppermute | solution.py:35
  45.6 9.7 %collective-permute-start.6 = (bf16[4,384,128]{2,1,0:T(8,128)(2,1)S(1)}, bf16[4,384,128]{2,1,0:T(8,128)(2,1)S(1)}, u32[]{:S(2)}, u32[]{:S(2)}) collective-permute-start(bf16[4,384,128]{2,1,0:T(8,128)(2,1)S(1)} %collective-permute-done.5.refs_1_.refs_2_), channel_id=1, source_target_pairs={{0,448},{64,0},{128,64},{192,128},{256,192},{320,256},{384,320},{4... | collective-permute-start | bytes 1179656 | tf_op jit(solution)/shard_map/ppermute | solution.py:35
  53.4 9.7 %collective-permute-start.3 = (bf16[4,384,128]{2,1,0:T(8,128)(2,1)S(1)}, bf16[4,384,128]{2,1,0:T(8,128)(2,1)S(1)}, u32[]{:S(2)}, u32[]{:S(2)}) collective-permute-start(bf16[4,384,128]{2,1,0:T(8,128)(2,1)S(1)} %collective-permute-done.2.refs_0_.refs_5_), channel_id=1, source_target_pairs={{0,64},{64,128},{128,192},{192,256},{256,320},{320,384},{384,448},... | collective-permute-start | bytes 1179656 | tf_op jit(solution)/shard_map/ppermute | solution.py:35
  64.7 18.3 %all-to-all-start = ((bf16[16,32,128]{2,1,0:T(8,128)(2,1)}), bf16[16,32,128]{2,1,0:T(8,128)(2,1)S(1)}, u32[]{:S(2)}, u32[]{:S(2)}) async-start(bf16[16,32,128]{2,1,0:T(8,128)(2,1)} %bitcast.10), calls=%async_computation | async-start | bytes 262144 | tf_op jit(solution)/shard_map/all_to_all | solution.py:215

commit v4 on v3

--- a/solution.py
+++ b/solution.py
@@ -150,15 +150,13 @@
         z = lax.div(inside, NEW // PAGE)
         first = pl.multiple_of(lax.rem(inside, NEW // PAGE) * PAGE, PAGE)
         keep = row < length - page * PAGE
-        for d in range(Y):
-
-            @pl.when(away == d)
-            def _():
-                for half in range(2):
-                    rows = blocks[d][z, pl.ds(half * NEW + first, PAGE), :]
-                    rows = jnp.where(keep, rows.astype(jnp.float32), 0.0).astype(jnp.bfloat16)
-                    for core in range(2):
-                        o_ref[k, core, half * PAGE : (half + 1) * PAGE, :] = rows
+        for half in range(2):
+            rows = blocks[0][z, pl.ds(half * NEW + first, PAGE), :]
+            for d in range(1, Y):
+                rows = jnp.where(away == d, blocks[d][z, pl.ds(half * NEW + first, PAGE), :], rows)
+            rows = jnp.where(keep, rows.astype(jnp.float32), 0.0).astype(jnp.bfloat16)
+            for core in range(2):
+                o_ref[k, core, half * PAGE : (half + 1) * PAGE, :] = rows
 
 
 def pick(scal, pages, blocks):
@@ -203,21 +201,21 @@
     column = lax.all_gather(mine, "zh", axis=0)
     a, b = [column], [column]
     for _ in range(3):
-        a.append(shift(a[-1], ("y",), (1,), (Y,)))
-        b.append(shift(b[-1], ("y",), (-1,), (Y,)))
-    far = shift(a[3], ("y",), (1,), (Y,))
+        a.append(shift(a[-1], ("y",), (-1,), (Y,)))
+        b.append(shift(b[-1], ("y",), (1,), (Y,)))
+    far = shift(a[3], ("y",), (-1,), (Y,))
 
     slots_here = ctx * tps + jnp.arange(tps, dtype=jnp.int32)
     page_ids = jnp.arange(slots.shape[1], dtype=jnp.int32)
     pages = jnp.sum(jnp.where(slots[0][None, :] == slots_here[:, None], page_ids[None, :], 0), axis=1)
-    by_distance = [column, b[1], b[2], b[3], far, a[3], a[2], a[1]]
+    by_distance = [column, a[1], a[2], a[3], far, b[3], b[2], b[1]]
     sent = pick(scal, pages, by_distance).reshape(2 * tps, 2 * PAGE, HEAD)
     got = lax.all_to_all(sent, ("x", "zl", "core"), split_axis=0, concat_axis=0, tiled=True)
     pools = assemble(core[None], got.reshape(tps, 2, 2 * PAGE, HEAD))
 
     state = attend(scal, q[0], [column], (0,))
     for away in (1, 2, 3):
-        state = attend(scal, q[0], [a[away], b[away]], (-away, away), state)
+        state = attend(scal, q[0], [a[away], b[away]], (away, -away), state)
     out = attend(scal, q[0], [far], (4,), state, last=True)
     return (out[None], *pools)
 

time: 84.2 us -> 82.9 us (0.985)
  waiting for transfers between devices: 16.9 us -> 6.66 us
  Pallas kernels: 8.92 us -> 14.1 us
  starting transfers between devices: 34 us -> 37.8 us
    ppermute x7, waiting for transfers between devices: 12.1 us -> 2.79 us  [shift(): return lax.ppermute(value, axes, [(i, moved(i)) for i in range(count)])]
    pallas_call x5, Pallas kernels: 6.64 us -> 12.1 us  [attend(): pl.pallas_call(functools.partial(attend_kernel, apart=apart, first=first,...]
    ppermute x7, starting transfers between devices: 21.9 us -> 26.1 us  [shift(): return lax.ppermute(value, axes, [(i, moved(i)) for i in range(count)])]
    all_to_all x1, waiting for transfers between devices: 4.79 us -> 3.88 us  [body(): lax.all_to_all(sent, ('x', 'zl', 'core'), split_axis=0, concat_axis=0, ti...]
  transfers between devices with their start and end apart: 8 -> 8, of which waited for: 5 -> 4; matrix products, arithmetic and copies ran while one was open for 0% -> 0% of each run, Pallas kernels for 8% -> 15%
where the time goes in v4:
time: 82.9 us; the launch traced here: 82.4 us
  starting transfers between devices  37.8 us (46%)
  blocking collectives  20 us (24%)
  Pallas kernels  14.1 us (17%)
  waiting for transfers between devices  6.66 us (8%)
  between operations  2.08 us (3%)
  other arithmetic  1.08 us (1%)
    ppermute x7, starting transfers between devices, shift(): return lax.ppermute(value, axes, [(i, moved(i)) for i in range(count)])  26.1 us
    all_gather x1, blocking collectives, body(): column = lax.all_gather(mine, 'zh', axis=0)  20 us
    pallas_call x5, Pallas kernels, attend(): pl.pallas_call(functools.partial(attend_kernel, apart=apart, first=first,...  12.1 us
    all_to_all x1, starting transfers between devices, body(): lax.all_to_all(sent, ('x', 'zl', 'core'), split_axis=0, concat_axis=0, ti...  11.7 us
    all_to_all x1, waiting for transfers between devices, body(): lax.all_to_all(sent, ('x', 'zl', 'core'), split_axis=0, concat_axis=0, ti...  3.88 us
    ppermute x7, waiting for transfers between devices, shift(): return lax.ppermute(value, axes, [(i, moved(i)) for i in range(count)])  2.79 us
  transfers between devices with their start and end apart: 8, of which 4 were waited for; matrix products, arithmetic and copies ran while one was open for 0% of the time, Pallas kernels for 15%

profile of v4, /device:TPU:1, one launch (start us, length us, event | category | flops | bytes accessed | tf_op | source)
XLA Modules:
  0.0 82.4 jit_solution(5609585752170390440)
XLA Ops:
  0.6 0.8 pad_maximum_fusion
  1.5 20.0 %all-gather = bf16[1536,128]{1,0:T(8,128)(2,1)S(1)} all-gather(bf16[384,128]{1,0:T(8,128)(2,1)S(1)} %pad_maximum_fusion), channel_id=2, replica_groups=mesh['y'=8,'zh'=4,'x'=4,'zl'=2,'core'=2] {'zh'}, dimensions={0}, use_global_device_ids=true | all-gather | bytes 491520 | tf_op jit(solution)/shard_map/all_gather | solution.py:201
  21.5 5.1 %collective-permute-start = (bf16[4,384,128]{2,1,0:T(8,128)(2,1)S(1)}, bf16[4,384,128]{2,1,0:T(8,128)(2,1)S(1)}, u32[]{:S(2)}, u32[]{:S(2)}) collective-permute-start(bf16[4,384,128]{2,1,0:T(8,128)(2,1)S(1)} %bitcast.12), channel_id=1, source_target_pairs={{0,448},{64,0},{128,64},{192,128},{256,192},{320,256},{384,320},{4... | collective-permute-start | bytes 1179656 | tf_op jit(solution)/shard_map/ppermute | solution.py:35
  26.6 1.9 %collective-permute-start.4 = (bf16[4,384,128]{2,1,0:T(8,128)(2,1)S(1)}, bf16[4,384,128]{2,1,0:T(8,128)(2,1)S(1)}, u32[]{:S(2)}, u32[]{:S(2)}) collective-permute-start(bf16[4,384,128]{2,1,0:T(8,128)(2,1)S(1)} %bitcast.13), channel_id=1, source_target_pairs={{0,64},{64,128},{128,192},{192,256},{256,320},{320,384},{384,448},... | collective-permute-start | bytes 1179656 | tf_op jit(solution)/shard_map/ppermute | solution.py:35
  29.8 0.7 copy-done.1
  30.5 0.2 select_reduce_fusion.pages
  30.7 0.1 pad_add_fusion.scal
  30.8 2.2 %attend_blocks.5 = (f32[1024,128]{1,0:T(8,128)S(1)}, f32[1024,256]{1,0:T(8,128)S(1)}) custom-call(s32[3]{0:T(128)S(1)} %pad_add_fusion.scal, bf16[128,1024]{1,0:T(8,128)(2,1)S(1)} %bitcast.17, bf16[4,384,128]{2,1,0:T(8,128)(2,1)S(1)} %bitcast.14), custom_call_target="tpu_custom_call" | custom-call | flops 4026531840 | bytes 393216 | tf_op jit(solution)/shard_map/attend_blocks/pallas_call | solution.py:121
  33.0 4.6 %collective-permute-start.1 = (bf16[4,384,128]{2,1,0:T(8,128)(2,1)S(1)}, bf16[4,384,128]{2,1,0:T(8,128)(2,1)S(1)}, u32[]{:S(2)}, u32[]{:S(2)}) collective-permute-start(bf16[4,384,128]{2,1,0:T(8,128)(2,1)S(1)} %collective-permute-done.refs_0_.refs_1_), channel_id=1, source_target_pairs={{0,448},{64,0},{128,64},{192,128},{256,192},{320,256},{384,320},{4... | collective-permute-start | bytes 1179656 | tf_op jit(solution)/shard_map/ppermute | solution.py:35
  37.6 1.9 %collective-permute-start.5 = (bf16[4,384,128]{2,1,0:T(8,128)(2,1)S(1)}, bf16[4,384,128]{2,1,0:T(8,128)(2,1)S(1)}, u32[]{:S(2)}, u32[]{:S(2)}) collective-permute-start(bf16[4,384,128]{2,1,0:T(8,128)(2,1)S(1)} %collective-permute-done.4.refs_1_.refs_7_), channel_id=1, source_target_pairs={{0,64},{64,128},{128,192},{192,256},{256,320},{320,384},{384,448},... | collective-permute-start | bytes 1179656 | tf_op jit(solution)/shard_map/ppermute | solution.py:35
  39.5 2.4 %attend_blocks.6 = (f32[1024,128]{1,0:T(8,128)S(1)}, f32[1024,256]{1,0:T(8,128)S(1)}) custom-call(s32[3]{0:T(128)S(1)} %pad_add_fusion.scal, bf16[128,1024]{1,0:T(8,128)(2,1)S(1)} %bitcast.18, bf16[4,384,128]{2,1,0:T(8,128)(2,1)S(1)} %collective-permute-done.refs_0_.refs_1_, ...), custom_call_target="tpu_custom_call", output_to_operand_aliasing={{0}: (4, {}), {1}: (5, {})} | custom-call | flops 8053063680 | bytes 786432 | tf_op jit(solution)/shard_map/attend_blocks/pallas_call | solution.py:121
  41.9 0.6 collective-permute-done.1.refs_0_.refs_2_
  42.5 5.1 %collective-permute-start.2 = (bf16[4,384,128]{2,1,0:T(8,128)(2,1)S(1)}, bf16[4,384,128]{2,1,0:T(8,128)(2,1)S(1)}, u32[]{:S(2)}, u32[]{:S(2)}) collective-permute-start(bf16[4,384,128]{2,1,0:T(8,128)(2,1)S(1)} %collective-permute-done.1.refs_0_.refs_2_), channel_id=1, source_target_pairs={{0,448},{64,0},{128,64},{192,128},{256,192},{320,256},{384,320},{4... | collective-permute-start | bytes 1179656 | tf_op jit(solution)/shard_map/ppermute | solution.py:35
  47.7 1.9 %collective-permute-start.6 = (bf16[4,384,128]{2,1,0:T(8,128)(2,1)S(1)}, bf16[4,384,128]{2,1,0:T(8,128)(2,1)S(1)}, u32[]{:S(2)}, u32[]{:S(2)}) collective-permute-start(bf16[4,384,128]{2,1,0:T(8,128)(2,1)S(1)} %collective-permute-done.5.refs_1_.refs_6_), channel_id=1, source_target_pairs={{0,64},{64,128},{128,192},{192,256},{256,320},{320,384},{384,448},... | collective-permute-start | bytes 1179656 | tf_op jit(solution)/shard_map/ppermute | solution.py:35
  49.6 2.6 %attend_blocks.7 = (f32[1024,128]{1,0:T(8,128)S(1)}, f32[1024,256]{1,0:T(8,128)S(1)}) custom-call(s32[3]{0:T(128)S(1)} %pad_add_fusion.scal, bf16[128,1024]{1,0:T(8,128)(2,1)S(1)} %bitcast.19, bf16[4,384,128]{2,1,0:T(8,128)(2,1)S(1)} %collective-permute-done.1.refs_0_.refs_2_, ...), custom_call_target="tpu_custom_call", output_to_operand_aliasing={{0}: (4, {}), {1}: (5, {})} | custom-call | flops 8053063680 | bytes 786432 | tf_op jit(solution)/shard_map/attend_blocks/pallas_call | solution.py:121
  52.2 0.2 collective-permute-done.2.refs_0_.refs_3_
  52.4 5.5 %collective-permute-start.3 = (bf16[4,384,128]{2,1,0:T(8,128)(2,1)S(1)}, bf16[4,384,128]{2,1,0:T(8,128)(2,1)S(1)}, u32[]{:S(2)}, u32[]{:S(2)}) collective-permute-start(bf16[4,384,128]{2,1,0:T(8,128)(2,1)S(1)} %collective-permute-done.2.refs_0_.refs_3_), channel_id=1, source_target_pairs={{0,448},{64,0},{128,64},{192,128},{256,192},{320,256},{384,320},{4... | collective-permute-start | bytes 1179656 | tf_op jit(solution)/shard_map/ppermute | solution.py:35
  57.9 2.6 %attend_blocks.8 = (f32[1024,128]{1,0:T(8,128)S(1)}, f32[1024,256]{1,0:T(8,128)S(1)}) custom-call(s32[3]{0:T(128)S(1)} %pad_add_fusion.scal, bf16[128,1024]{1,0:T(8,128)(2,1)S(1)} %bitcast.20, bf16[4,384,128]{2,1,0:T(8,128)(2,1)S(1)} %collective-permute-done.2.refs_0_.refs_3_, ...), custom_call_target="tpu_custom_call", output_to_operand_aliasing={{0}: (4, {}), {1}: (5, {})} | custom-call | flops 8053063680 | bytes 786432 | tf_op jit(solution)/shard_map/attend_blocks/pallas_call | solution.py:121
  60.5 2.0 %collective-permute-done.3.refs_0_.refs_4_ = bf16[4,384,128]{2,1,0:T(8,128)(2,1)S(1)} collective-permute-done((bf16[4,384,128]{2,1,0:T(8,128)(2,1)S(1)}, bf16[4,384,128]{2,1,0:T(8,128)(2,1)S(1)}, u32[]{:S(2)}, u32[]{:S(2)}) %collective-permute-start.3) | collective-permute-done | bytes 393248 | tf_op jit(solution)/shard_map/ppermute | solution.py:35
  62.6 1.4 %pick_pages.1 = bf16[8,2,32,128]{3,2,1,0:T(8,128)(2,1)} custom-call(s32[3]{0:T(128)S(1)} %pad_add_fusion.scal, s32[8]{0:T(128)S(1)} %select_reduce_fusion.pages, bf16[4,384,128]{2,1,0:T(8,128)(2,1)S(1)} %bitcast.15, bf16[4,384,128]{2,1,0:T(8,128)(2,1)S(1)} %collective-permute-done.refs_0_.refs_1_, ...), custom_call_target="tpu_custom_call" | custom-call | tf_op jit(solution)/shard_map/pick_pages/pallas_call | solution.py:165
  63.9 11.7 %all-to-all-start = ((bf16[16,32,128]{2,1,0:T(8,128)(2,1)}), bf16[16,32,128]{2,1,0:T(8,128)(2,1)S(1)}, u32[]{:S(2)}, u32[]{:S(2)}) async-start(bf16[16,32,128]{2,1,0:T(8,128)(2,1)} %bitcast.10), calls=%async_computation | async-start | bytes 262144 | tf_op jit(solution)/shard_map/all_to_all | solution.py:213
  75.6 2.3 %attend_blocks.9 = bf16[128,1024]{1,0:T(8,128)(2,1)} custom-call(s32[3]{0:T(128)S(1)} %pad_add_fusion.scal, bf16[128,1024]{1,0:T(8,128)(2,1)S(1)} %bitcast.21, bf16[4,384,128]{2,1,0:T(8,128)(2,1)S(1)} %collective-permute-done.3.refs_0_.refs_4_, f32[1024,128]{1,0:T(8,128)S(1)} %get-tuple-element.19.refs_1_, f32[1024,256]{1,0:T(8,128)S(1)} %get-tuple-element.20.refs_2_), custom_call_target="tpu_custom_call" | custom-call | flops 4026531840 | bytes 393216 | tf_op jit(solution)/shard_map/attend_blocks/pallas_call | solution.py:121
  77.9 3.9 %all-to-all-done = bf16[16,32,128]{2,1,0:T(8,128)(2,1)S(1)} async-done(((bf16[16,32,128]{2,1,0:T(8,128)(2,1)}), bf16[16,32,128]{2,1,0:T(8,128)(2,1)S(1)}, u32[]{:S(2)}, u32[]{:S(2)}) %all-to-all-start) | async-done | bytes 131104 | tf_op jit(solution)/shard_map/all_to_all | solution.py:213
  81.8 0.6 assemble_pages.1
  (8 shorter events, 0.0 us)
Async XLA Ops:
  1.4 29.3 %copy-start = (bf16[1,128,1024]{2,1,0:T(8,128)(2,1)S(1)}, bf16[1,128,1024]{2,1,0:T(8,128)(2,1)}, u32[]{:S(2)}) copy-start(bf16[1,128,1024]{2,1,0:T(8,128)(2,1)} %param.8) | copy-start | bytes 786436
  21.5 11.5 %collective-permute-start = (bf16[4,384,128]{2,1,0:T(8,128)(2,1)S(1)}, bf16[4,384,128]{2,1,0:T(8,128)(2,1)S(1)}, u32[]{:S(2)}, u32[]{:S(2)}) collective-permute-start(bf16[4,384,128]{2,1,0:T(8,128)(2,1)S(1)} %bitcast.12), channel_id=1, source_target_pairs={{0,448},{64,0},{128,64},{192,128},{256,192},{320,256},{384,320},{4... | collective-permute-start | bytes 1179656 | tf_op jit(solution)/shard_map/ppermute | solution.py:35
  26.6 11.0 %collective-permute-start.4 = (bf16[4,384,128]{2,1,0:T(8,128)(2,1)S(1)}, bf16[4,384,128]{2,1,0:T(8,128)(2,1)S(1)}, u32[]{:S(2)}, u32[]{:S(2)}) collective-permute-start(bf16[4,384,128]{2,1,0:T(8,128)(2,1)S(1)} %bitcast.13), channel_id=1, source_target_pairs={{0,64},{64,128},{128,192},{192,256},{256,320},{320,384},{384,448},... | collective-permute-start | bytes 1179656 | tf_op jit(solution)/shard_map/ppermute | solution.py:35
  29.8 0.7 copy-start.1
  33.0 9.5 %collective-permute-start.1 = (bf16[4,384,128]{2,1,0:T(8,128)(2,1)S(1)}, bf16[4,384,128]{2,1,0:T(8,128)(2,1)S(1)}, u32[]{:S(2)}, u32[]{:S(2)}) collective-permute-start(bf16[4,384,128]{2,1,0:T(8,128)(2,1)S(1)} %collective-permute-done.refs_0_.refs_1_), channel_id=1, source_target_pairs={{0,448},{64,0},{128,64},{192,128},{256,192},{320,256},{384,320},{4... | collective-permute-start | bytes 1179656 | tf_op jit(solution)/shard_map/ppermute | solution.py:35
  37.6 10.1 %collective-permute-start.5 = (bf16[4,384,128]{2,1,0:T(8,128)(2,1)S(1)}, bf16[4,384,128]{2,1,0:T(8,128)(2,1)S(1)}, u32[]{:S(2)}, u32[]{:S(2)}) collective-permute-start(bf16[4,384,128]{2,1,0:T(8,128)(2,1)S(1)} %collective-permute-done.4.refs_1_.refs_7_), channel_id=1, source_target_pairs={{0,64},{64,128},{128,192},{192,256},{256,320},{320,384},{384,448},... | collective-permute-start | bytes 1179656 | tf_op jit(solution)/shard_map/ppermute | solution.py:35
  42.5 9.9 %collective-permute-start.2 = (bf16[4,384,128]{2,1,0:T(8,128)(2,1)S(1)}, bf16[4,384,128]{2,1,0:T(8,128)(2,1)S(1)}, u32[]{:S(2)}, u32[]{:S(2)}) collective-permute-start(bf16[4,384,128]{2,1,0:T(8,128)(2,1)S(1)} %collective-permute-done.1.refs_0_.refs_2_), channel_id=1, source_target_pairs={{0,448},{64,0},{128,64},{192,128},{256,192},{320,256},{384,320},{4... | collective-permute-start | bytes 1179656 | tf_op jit(solution)/shard_map/ppermute | solution.py:35
  47.7 10.2 %collective-permute-start.6 = (bf16[4,384,128]{2,1,0:T(8,128)(2,1)S(1)}, bf16[4,384,128]{2,1,0:T(8,128)(2,1)S(1)}, u32[]{:S(2)}, u32[]{:S(2)}) collective-permute-start(bf16[4,384,128]{2,1,0:T(8,128)(2,1)S(1)} %collective-permute-done.5.refs_1_.refs_6_), channel_id=1, source_target_pairs={{0,64},{64,128},{128,192},{192,256},{256,320},{320,384},{384,448},... | collective-permute-start | bytes 1179656 | tf_op jit(solution)/shard_map/ppermute | solution.py:35
  52.4 10.2 %collective-permute-start.3 = (bf16[4,384,128]{2,1,0:T(8,128)(2,1)S(1)}, bf16[4,384,128]{2,1,0:T(8,128)(2,1)S(1)}, u32[]{:S(2)}, u32[]{:S(2)}) collective-permute-start(bf16[4,384,128]{2,1,0:T(8,128)(2,1)S(1)} %collective-permute-done.2.refs_0_.refs_3_), channel_id=1, source_target_pairs={{0,448},{64,0},{128,64},{192,128},{256,192},{320,256},{384,320},{4... | collective-permute-start | bytes 1179656 | tf_op jit(solution)/shard_map/ppermute | solution.py:35
  63.9 17.8 %all-to-all-start = ((bf16[16,32,128]{2,1,0:T(8,128)(2,1)}), bf16[16,32,128]{2,1,0:T(8,128)(2,1)S(1)}, u32[]{:S(2)}, u32[]{:S(2)}) async-start(bf16[16,32,128]{2,1,0:T(8,128)(2,1)} %bitcast.10), calls=%async_computation | async-start | bytes 262144 | tf_op jit(solution)/shard_map/all_to_all | solution.py:213

commit v5 on v4

--- a/solution.py
+++ b/solution.py
@@ -36,7 +36,8 @@
 
 
 def attend_kernel(scal, q_ref, *refs, apart, first, last):
-    count = len(apart)
+    split = last
+    count = len(apart) + split
     blocks, refs = refs[:count], refs[count:]
     if not first:
         m_ref, acc_ref, *refs = refs
@@ -54,12 +55,14 @@
     heads = tile // NEW
 
     def step(i, j, masked, with_new=True):
+        new_ref, old_ref = blocks[i], blocks[-1] if split else blocks[i]
+        at = 0 if split else 2 * NEW
         new_keys = STEP_NEW if with_new else 0
         width = new_keys + STEP_OLD
-        k = [blocks[i][z, 0:NEW, :] for z in range(Z)] if with_new else []
-        k += [blocks[i][z, 2 * NEW : 2 * NEW + OLD, :] for z in range(Z)]
-        v = [blocks[i][z, NEW : 2 * NEW, :] for z in range(Z)] if with_new else []
-        v += [blocks[i][z, 2 * NEW + OLD : ROWS, :] for z in range(Z)]
+        k = [new_ref[z, 0:NEW, :] for z in range(Z)] if with_new else []
+        k += [old_ref[z, at : at + OLD, :] for z in range(Z)]
+        v = [new_ref[z, NEW : 2 * NEW, :] for z in range(Z)] if with_new else []
+        v += [old_ref[z, at + OLD : at + 2 * OLD, :] for z in range(Z)]
         k, v = jnp.concatenate(k, axis=0), jnp.concatenate(v, axis=0)
         v = jnp.concatenate([v, jnp.ones_like(v)], axis=1)
 
@@ -116,8 +119,8 @@
         jax.ShapeDtypeStruct((HEADS * NEW, HEAD), jnp.float32),
         jax.ShapeDtypeStruct((HEADS * NEW, 2 * HEAD), jnp.float32),
     )
-    first, count = state is None, len(apart)
-    keys = count * (STEP_NEW + STEP_OLD)
+    first, count = state is None, len(blocks)
+    keys = len(apart) * (STEP_NEW + STEP_OLD)
     return pl.pallas_call(
         functools.partial(attend_kernel, apart=apart, first=first, last=last),
         in_specs=[pl.BlockSpec(memory_space=pltpu.SMEM), whole]
@@ -129,7 +132,7 @@
         compiler_params=pltpu.CompilerParams(vmem_limit_bytes=24 << 20),
         cost_estimate=pl.CostEstimate(
             flops=COST * HEADS * NEW * keys * HEAD,
-            bytes_accessed=count * Z * ROWS * HEAD * 2,
+            bytes_accessed=len(apart) * Z * ROWS * HEAD * 2,
             transcendentals=HEADS * NEW * keys,
         ),
         name="attend_blocks",
@@ -203,12 +206,12 @@
     for _ in range(3):
         a.append(shift(a[-1], ("y",), (-1,), (Y,)))
         b.append(shift(b[-1], ("y",), (1,), (Y,)))
-    far = shift(a[3], ("y",), (-1,), (Y,))
+    far = [shift(part, ("y",), (-1,), (Y,)) for part in (a[3][:, : 2 * NEW], a[3][:, 2 * NEW :])]
 
     slots_here = ctx * tps + jnp.arange(tps, dtype=jnp.int32)
     page_ids = jnp.arange(slots.shape[1], dtype=jnp.int32)
     pages = jnp.sum(jnp.where(slots[0][None, :] == slots_here[:, None], page_ids[None, :], 0), axis=1)
-    by_distance = [column, a[1], a[2], a[3], far, b[3], b[2], b[1]]
+    by_distance = [column, a[1], a[2], a[3], far[0], b[3], b[2], b[1]]
     sent = pick(scal, pages, by_distance).reshape(2 * tps, 2 * PAGE, HEAD)
     got = lax.all_to_all(sent, ("x", "zl", "core"), split_axis=0, concat_axis=0, tiled=True)
     pools = assemble(core[None], got.reshape(tps, 2, 2 * PAGE, HEAD))
@@ -216,7 +219,7 @@
     state = attend(scal, q[0], [column], (0,))
     for away in (1, 2, 3):
         state = attend(scal, q[0], [a[away], b[away]], (away, -away), state)
-    out = attend(scal, q[0], [far], (4,), state, last=True)
+    out = attend(scal, q[0], far, (4,), state, last=True)
     return (out[None], *pools)
 
 

time: 82.9 us -> 83.7 us (level)
  the two profiles are of different devices: /device:TPU:1 before, /device:TPU:137 now
where the time goes in v5:
time: 83.7 us; the launch traced here: 83.1 us
  starting transfers between devices  44.9 us (54%)
  blocking collectives  15.9 us (19%)
  Pallas kernels  10.1 us (12%)
  waiting for transfers between devices  8.41 us (10%)
  between operations  2.11 us (3%)
  other arithmetic  1.08 us (1%)
    ppermute x8, starting transfers between devices, shift(): return lax.ppermute(value, axes, [(i, moved(i)) for i in range(count)])  26.3 us
    all_to_all x1, starting transfers between devices, body(): lax.all_to_all(sent, ('x', 'zl', 'core'), split_axis=0, concat_axis=0, ti...  18.6 us
    all_gather x1, blocking collectives, body(): column = lax.all_gather(mine, 'zh', axis=0)  15.9 us
    pallas_call x5, Pallas kernels, attend(): pl.pallas_call(functools.partial(attend_kernel, apart=apart, first=first,...  8.07 us
    all_to_all x1, waiting for transfers between devices, body(): lax.all_to_all(sent, ('x', 'zl', 'core'), split_axis=0, concat_axis=0, ti...  4.78 us
    ppermute x8, waiting for transfers between devices, shift(): return lax.ppermute(value, axes, [(i, moved(i)) for i in range(count)])  3.62 us
  transfers between devices with their start and end apart: 9, of which 2 were waited for; matrix products, arithmetic and copies ran while one was open for 0% of the time, Pallas kernels for 11%

profile of v5, /device:TPU:137, one launch (start us, length us, event | category | flops | bytes accessed | tf_op | source)
XLA Modules:
  0.0 83.1 jit_solution(4550058497369369622)
XLA Ops:
  0.6 0.8 pad_maximum_fusion
  1.5 15.9 %all-gather = bf16[1536,128]{1,0:T(8,128)(2,1)S(1)} all-gather(bf16[384,128]{1,0:T(8,128)(2,1)S(1)} %pad_maximum_fusion), channel_id=2, replica_groups=mesh['y'=8,'zh'=4,'x'=4,'zl'=2,'core'=2] {'zh'}, dimensions={0}, use_global_device_ids=true | all-gather | bytes 491520 | tf_op jit(solution)/shard_map/all_gather | solution.py:204
  17.3 2.1 %collective-permute-start = (bf16[4,384,128]{2,1,0:T(8,128)(2,1)S(1)}, bf16[4,384,128]{2,1,0:T(8,128)(2,1)S(1)}, u32[]{:S(2)}, u32[]{:S(2)}) collective-permute-start(bf16[4,384,128]{2,1,0:T(8,128)(2,1)S(1)} %bitcast.12), channel_id=1, source_target_pairs={{0,448},{64,0},{128,64},{192,128},{256,192},{320,256},{384,320},{4... | collective-permute-start | bytes 1179656 | tf_op jit(solution)/shard_map/ppermute | solution.py:35
  19.4 3.2 %collective-permute-start.5 = (bf16[4,384,128]{2,1,0:T(8,128)(2,1)S(1)}, bf16[4,384,128]{2,1,0:T(8,128)(2,1)S(1)}, u32[]{:S(2)}, u32[]{:S(2)}) collective-permute-start(bf16[4,384,128]{2,1,0:T(8,128)(2,1)S(1)} %bitcast.13), channel_id=1, source_target_pairs={{0,64},{64,128},{128,192},{192,256},{256,320},{320,384},{384,448},... | collective-permute-start | bytes 1179656 | tf_op jit(solution)/shard_map/ppermute | solution.py:35
  23.9 0.7 copy-done.1
  24.6 0.2 select_reduce_fusion.pages
  24.8 0.1 pad_add_fusion.scal
  24.9 2.2 %attend_blocks.5 = (f32[1024,128]{1,0:T(8,128)S(1)}, f32[1024,256]{1,0:T(8,128)S(1)}) custom-call(s32[3]{0:T(128)S(1)} %pad_add_fusion.scal, bf16[128,1024]{1,0:T(8,128)(2,1)S(1)} %bitcast.17, bf16[4,384,128]{2,1,0:T(8,128)(2,1)S(1)} %bitcast.14), custom_call_target="tpu_custom_call" | custom-call | flops 4026531840 | bytes 393216 | tf_op jit(solution)/shard_map/attend_blocks/pallas_call | solution.py:124
  27.1 3.8 %collective-permute-start.1 = (bf16[4,384,128]{2,1,0:T(8,128)(2,1)S(1)}, bf16[4,384,128]{2,1,0:T(8,128)(2,1)S(1)}, u32[]{:S(2)}, u32[]{:S(2)}) collective-permute-start(bf16[4,384,128]{2,1,0:T(8,128)(2,1)S(1)} %collective-permute-done.refs_0_.refs_1_), channel_id=1, source_target_pairs={{0,448},{64,0},{128,64},{192,128},{256,192},{320,256},{384,320},{4... | collective-permute-start | bytes 1179656 | tf_op jit(solution)/shard_map/ppermute | solution.py:35
  30.9 1.9 %collective-permute-start.6 = (bf16[4,384,128]{2,1,0:T(8,128)(2,1)S(1)}, bf16[4,384,128]{2,1,0:T(8,128)(2,1)S(1)}, u32[]{:S(2)}, u32[]{:S(2)}) collective-permute-start(bf16[4,384,128]{2,1,0:T(8,128)(2,1)S(1)} %collective-permute-done.5.refs_1_.refs_7_), channel_id=1, source_target_pairs={{0,64},{64,128},{128,192},{192,256},{256,320},{320,384},{384,448},... | collective-permute-start | bytes 1179656 | tf_op jit(solution)/shard_map/ppermute | solution.py:35
  32.8 2.9 %attend_blocks.6 = (f32[1024,128]{1,0:T(8,128)S(1)}, f32[1024,256]{1,0:T(8,128)S(1)}) custom-call(s32[3]{0:T(128)S(1)} %pad_add_fusion.scal, bf16[128,1024]{1,0:T(8,128)(2,1)S(1)} %bitcast.18, bf16[4,384,128]{2,1,0:T(8,128)(2,1)S(1)} %collective-permute-done.refs_0_.refs_1_, ...), custom_call_target="tpu_custom_call", output_to_operand_aliasing={{0}: (4, {}), {1}: (5, {})} | custom-call | flops 8053063680 | bytes 786432 | tf_op jit(solution)/shard_map/attend_blocks/pallas_call | solution.py:124
  35.8 3.9 %collective-permute-start.2 = (bf16[4,384,128]{2,1,0:T(8,128)(2,1)S(1)}, bf16[4,384,128]{2,1,0:T(8,128)(2,1)S(1)}, u32[]{:S(2)}, u32[]{:S(2)}) collective-permute-start(bf16[4,384,128]{2,1,0:T(8,128)(2,1)S(1)} %collective-permute-done.1.refs_0_.refs_2_), channel_id=1, source_target_pairs={{0,448},{64,0},{128,64},{192,128},{256,192},{320,256},{384,320},{4... | collective-permute-start | bytes 1179656 | tf_op jit(solution)/shard_map/ppermute | solution.py:35
  39.7 0.0 collective-permute-done.6.refs_1_.refs_6_
  39.7 2.1 %collective-permute-start.7 = (bf16[4,384,128]{2,1,0:T(8,128)(2,1)S(1)}, bf16[4,384,128]{2,1,0:T(8,128)(2,1)S(1)}, u32[]{:S(2)}, u32[]{:S(2)}) collective-permute-start(bf16[4,384,128]{2,1,0:T(8,128)(2,1)S(1)} %collective-permute-done.6.refs_1_.refs_6_), channel_id=1, source_target_pairs={{0,64},{64,128},{128,192},{192,256},{256,320},{320,384},{384,448},... | collective-permute-start | bytes 1179656 | tf_op jit(solution)/shard_map/ppermute | solution.py:35
  41.8 0.8 attend_blocks.7
  42.6 3.6 %collective-permute-done.2.refs_0_.refs_3_ = bf16[4,384,128]{2,1,0:T(8,128)(2,1)S(1)} collective-permute-done((bf16[4,384,128]{2,1,0:T(8,128)(2,1)S(1)}, bf16[4,384,128]{2,1,0:T(8,128)(2,1)S(1)}, u32[]{:S(2)}, u32[]{:S(2)}) %collective-permute-start.2) | collective-permute-done | bytes 393248 | tf_op jit(solution)/shard_map/ppermute | solution.py:35
  46.2 4.3 %collective-permute-start.3 = (bf16[4,256,128]{2,1,0:T(8,128)(2,1)S(1)}, bf16[4,256,128]{2,1,0:T(8,128)(2,1)S(1)}, u32[]{:S(2)}, u32[]{:S(2)}) collective-permute-start(bf16[4,256,128]{2,1,0:T(8,128)(2,1)S(1)} %slice.8), channel_id=1, source_target_pairs={{0,448},{64,0},{128,64},{192,128},{256,192},{320,256},{384,320},{4... | collective-permute-start | bytes 786440 | tf_op jit(solution)/shard_map/ppermute | solution.py:35
  50.5 5.0 %collective-permute-start.4 = (bf16[4,128,128]{2,1,0:T(8,128)(2,1)S(1)}, bf16[4,128,128]{2,1,0:T(8,128)(2,1)S(1)}, u32[]{:S(2)}, u32[]{:S(2)}) collective-permute-start(bf16[4,128,128]{2,1,0:T(8,128)(2,1)S(1)} %slice.9), channel_id=1, source_target_pairs={{0,448},{64,0},{128,64},{192,128},{256,192},{320,256},{384,320},{4... | collective-permute-start | bytes 393224 | tf_op jit(solution)/shard_map/ppermute | solution.py:35
  55.5 0.8 attend_blocks.8
  56.4 1.4 %pick_pages.1 = bf16[8,2,32,128]{3,2,1,0:T(8,128)(2,1)} custom-call(s32[3]{0:T(128)S(1)} %pad_add_fusion.scal, s32[8]{0:T(128)S(1)} %select_reduce_fusion.pages, bf16[4,384,128]{2,1,0:T(8,128)(2,1)S(1)} %bitcast.15, bf16[4,384,128]{2,1,0:T(8,128)(2,1)S(1)} %collective-permute-done.refs_0_.refs_1_, ...), custom_call_target="tpu_custom_call" | custom-call | tf_op jit(solution)/shard_map/pick_pages/pallas_call | solution.py:168
  57.7 18.6 %all-to-all-start = ((bf16[16,32,128]{2,1,0:T(8,128)(2,1)}), bf16[16,32,128]{2,1,0:T(8,128)(2,1)S(1)}, u32[]{:S(2)}, u32[]{:S(2)}) async-start(bf16[16,32,128]{2,1,0:T(8,128)(2,1)} %bitcast.10), calls=%async_computation | async-start | bytes 262144 | tf_op jit(solution)/shard_map/all_to_all | solution.py:216
  76.3 1.4 %attend_blocks.9 = bf16[128,1024]{1,0:T(8,128)(2,1)} custom-call(s32[3]{0:T(128)S(1)} %pad_add_fusion.scal, bf16[128,1024]{1,0:T(8,128)(2,1)S(1)} %bitcast.21, bf16[4,256,128]{2,1,0:T(8,128)(2,1)S(1)} %collective-permute-done.3.refs_0_.refs_4_, bf16[4,128,128]{2,1,0:T(8,128)(2,1)S(1)} %collective-permute-done.4.refs_1_, ...), custom_call_target="tpu_custom_call" | custom-call | flops 4026531840 | bytes 393216 | tf_op jit(solution)/shard_map/attend_blocks/pallas_call | solution.py:124
  77.7 4.8 %all-to-all-done = bf16[16,32,128]{2,1,0:T(8,128)(2,1)S(1)} async-done(((bf16[16,32,128]{2,1,0:T(8,128)(2,1)}), bf16[16,32,128]{2,1,0:T(8,128)(2,1)S(1)}, u32[]{:S(2)}, u32[]{:S(2)}) %all-to-all-start) | async-done | bytes 131104 | tf_op jit(solution)/shard_map/all_to_all | solution.py:216
  82.5 0.6 assemble_pages.1
  (12 shorter events, 0.1 us)
Async XLA Ops:
  1.4 23.4 %copy-start = (bf16[1,128,1024]{2,1,0:T(8,128)(2,1)S(1)}, bf16[1,128,1024]{2,1,0:T(8,128)(2,1)}, u32[]{:S(2)}) copy-start(bf16[1,128,1024]{2,1,0:T(8,128)(2,1)} %param.8) | copy-start | bytes 786436
  17.3 9.8 %collective-permute-start = (bf16[4,384,128]{2,1,0:T(8,128)(2,1)S(1)}, bf16[4,384,128]{2,1,0:T(8,128)(2,1)S(1)}, u32[]{:S(2)}, u32[]{:S(2)}) collective-permute-start(bf16[4,384,128]{2,1,0:T(8,128)(2,1)S(1)} %bitcast.12), channel_id=1, source_target_pairs={{0,448},{64,0},{128,64},{192,128},{256,192},{320,256},{384,320},{4... | collective-permute-start | bytes 1179656 | tf_op jit(solution)/shard_map/ppermute | solution.py:35
  19.4 11.5 %collective-permute-start.5 = (bf16[4,384,128]{2,1,0:T(8,128)(2,1)S(1)}, bf16[4,384,128]{2,1,0:T(8,128)(2,1)S(1)}, u32[]{:S(2)}, u32[]{:S(2)}) collective-permute-start(bf16[4,384,128]{2,1,0:T(8,128)(2,1)S(1)} %bitcast.13), channel_id=1, source_target_pairs={{0,64},{64,128},{128,192},{192,256},{256,320},{320,384},{384,448},... | collective-permute-start | bytes 1179656 | tf_op jit(solution)/shard_map/ppermute | solution.py:35
  23.9 0.7 copy-start.1
  27.1 8.7 %collective-permute-start.1 = (bf16[4,384,128]{2,1,0:T(8,128)(2,1)S(1)}, bf16[4,384,128]{2,1,0:T(8,128)(2,1)S(1)}, u32[]{:S(2)}, u32[]{:S(2)}) collective-permute-start(bf16[4,384,128]{2,1,0:T(8,128)(2,1)S(1)} %collective-permute-done.refs_0_.refs_1_), channel_id=1, source_target_pairs={{0,448},{64,0},{128,64},{192,128},{256,192},{320,256},{384,320},{4... | collective-permute-start | bytes 1179656 | tf_op jit(solution)/shard_map/ppermute | solution.py:35
  30.9 8.8 %collective-permute-start.6 = (bf16[4,384,128]{2,1,0:T(8,128)(2,1)S(1)}, bf16[4,384,128]{2,1,0:T(8,128)(2,1)S(1)}, u32[]{:S(2)}, u32[]{:S(2)}) collective-permute-start(bf16[4,384,128]{2,1,0:T(8,128)(2,1)S(1)} %collective-permute-done.5.refs_1_.refs_7_), channel_id=1, source_target_pairs={{0,64},{64,128},{128,192},{192,256},{256,320},{320,384},{384,448},... | collective-permute-start | bytes 1179656 | tf_op jit(solution)/shard_map/ppermute | solution.py:35
  35.8 10.4 %collective-permute-start.2 = (bf16[4,384,128]{2,1,0:T(8,128)(2,1)S(1)}, bf16[4,384,128]{2,1,0:T(8,128)(2,1)S(1)}, u32[]{:S(2)}, u32[]{:S(2)}) collective-permute-start(bf16[4,384,128]{2,1,0:T(8,128)(2,1)S(1)} %collective-permute-done.1.refs_0_.refs_2_), channel_id=1, source_target_pairs={{0,448},{64,0},{128,64},{192,128},{256,192},{320,256},{384,320},{4... | collective-permute-start | bytes 1179656 | tf_op jit(solution)/shard_map/ppermute | solution.py:35
  39.7 15.8 %collective-permute-start.7 = (bf16[4,384,128]{2,1,0:T(8,128)(2,1)S(1)}, bf16[4,384,128]{2,1,0:T(8,128)(2,1)S(1)}, u32[]{:S(2)}, u32[]{:S(2)}) collective-permute-start(bf16[4,384,128]{2,1,0:T(8,128)(2,1)S(1)} %collective-permute-done.6.refs_1_.refs_6_), channel_id=1, source_target_pairs={{0,64},{64,128},{128,192},{192,256},{256,320},{320,384},{384,448},... | collective-permute-start | bytes 1179656 | tf_op jit(solution)/shard_map/ppermute | solution.py:35
  46.2 10.2 %collective-permute-start.3 = (bf16[4,256,128]{2,1,0:T(8,128)(2,1)S(1)}, bf16[4,256,128]{2,1,0:T(8,128)(2,1)S(1)}, u32[]{:S(2)}, u32[]{:S(2)}) collective-permute-start(bf16[4,256,128]{2,1,0:T(8,128)(2,1)S(1)} %slice.8), channel_id=1, source_target_pairs={{0,448},{64,0},{128,64},{192,128},{256,192},{320,256},{384,320},{4... | collective-permute-start | bytes 786440 | tf_op jit(solution)/shard_map/ppermute | solution.py:35
  50.5 25.8 %collective-permute-start.4 = (bf16[4,128,128]{2,1,0:T(8,128)(2,1)S(1)}, bf16[4,128,128]{2,1,0:T(8,128)(2,1)S(1)}, u32[]{:S(2)}, u32[]{:S(2)}) collective-permute-start(bf16[4,128,128]{2,1,0:T(8,128)(2,1)S(1)} %slice.9), channel_id=1, source_target_pairs={{0,448},{64,0},{128,64},{192,128},{256,192},{320,256},{384,320},{4... | collective-permute-start | bytes 393224 | tf_op jit(solution)/shard_map/ppermute | solution.py:35
  57.7 24.7 %all-to-all-start = ((bf16[16,32,128]{2,1,0:T(8,128)(2,1)}), bf16[16,32,128]{2,1,0:T(8,128)(2,1)S(1)}, u32[]{:S(2)}, u32[]{:S(2)}) async-start(bf16[16,32,128]{2,1,0:T(8,128)(2,1)} %bitcast.10), calls=%async_computation | async-start | bytes 262144 | tf_op jit(solution)/shard_map/all_to_all | solution.py:216

commit v6 on v5

--- a/solution.py
+++ b/solution.py
@@ -146,7 +146,7 @@
     blocks, o_ref = refs[:Y], refs[Y]
     y, length = lax.div(scal[0], Z), scal[1]
     row = lax.broadcasted_iota(jnp.int32, (PAGE, HEAD), 0)
-    for k in range(o_ref.shape[0]):
+    for k in range(o_ref.shape[1]):
         page = pages[k]
         away = lax.rem(lax.div(page, PAGES) - y + Y, Y)
         inside = lax.rem(page, PAGES)
@@ -159,7 +159,7 @@
                 rows = jnp.where(away == d, blocks[d][z, pl.ds(half * NEW + first, PAGE), :], rows)
             rows = jnp.where(keep, rows.astype(jnp.float32), 0.0).astype(jnp.bfloat16)
             for core in range(2):
-                o_ref[k, core, half * PAGE : (half + 1) * PAGE, :] = rows
+                o_ref[core, k, half * PAGE : (half + 1) * PAGE, :] = rows
 
 
 def pick(scal, pages, blocks):
@@ -169,7 +169,7 @@
         pick_kernel,
         in_specs=[small, small] + [whole] * Y,
         out_specs=whole,
-        out_shape=jax.ShapeDtypeStruct((count, 2, 2 * PAGE, HEAD), jnp.bfloat16),
+        out_shape=jax.ShapeDtypeStruct((2, count, 2 * PAGE, HEAD), jnp.bfloat16),
         compiler_params=pltpu.CompilerParams(vmem_limit_bytes=8 << 20),
         name="pick_pages",
     )(scal, pages, *blocks)
@@ -177,13 +177,13 @@
 
 def assemble_kernel(core, got_ref, k_ref, v_ref):
     other = 1 - core[0]
-    for t in range(got_ref.shape[0]):
+    for t in range(got_ref.shape[1]):
         for half, out in enumerate((k_ref, v_ref)):
-            out[0, :, t * HEAD : (t + 1) * HEAD] = got_ref[t, other, half * PAGE : (half + 1) * PAGE, :]
+            out[0, :, t * HEAD : (t + 1) * HEAD] = got_ref[other, t, half * PAGE : (half + 1) * PAGE, :]
 
 
 def assemble(core, got):
-    tps = got.shape[0]
+    tps = got.shape[1]
     whole = pl.BlockSpec(memory_space=pltpu.VMEM)
     return pl.pallas_call(
         assemble_kernel,
@@ -213,8 +213,8 @@
     pages = jnp.sum(jnp.where(slots[0][None, :] == slots_here[:, None], page_ids[None, :], 0), axis=1)
     by_distance = [column, a[1], a[2], a[3], far[0], b[3], b[2], b[1]]
     sent = pick(scal, pages, by_distance).reshape(2 * tps, 2 * PAGE, HEAD)
-    got = lax.all_to_all(sent, ("x", "zl", "core"), split_axis=0, concat_axis=0, tiled=True)
-    pools = assemble(core[None], got.reshape(tps, 2, 2 * PAGE, HEAD))
+    got = lax.all_to_all(sent, ("core", "x", "zl"), split_axis=0, concat_axis=0, tiled=True)
+    pools = assemble(core[None], got.reshape(2, tps, 2 * PAGE, HEAD))
 
     state = attend(scal, q[0], [column], (0,))
     for away in (1, 2, 3):

time: 83.7 us -> 81.9 us (0.978)
  the two profiles are of different devices: /device:TPU:137 before, /device:TPU:1 now
where the time goes in v6:
time: 81.9 us; the launch traced here: 81.4 us
  starting transfers between devices  39.1 us (48%)
  blocking collectives  20 us (24%)
  Pallas kernels  14.1 us (17%)
  waiting for transfers between devices  4.26 us (5%)
  between operations  2.11 us (3%)
  other arithmetic  1.08 us (1%)
    ppermute x8, starting transfers between devices, shift(): return lax.ppermute(value, axes, [(i, moved(i)) for i in range(count)])  28 us
    all_gather x1, blocking collectives, body(): column = lax.all_gather(mine, 'zh', axis=0)  20 us
    pallas_call x5, Pallas kernels, attend(): pl.pallas_call(functools.partial(attend_kernel, apart=apart, first=first,...  12.1 us
    all_to_all x1, starting transfers between devices, body(): lax.all_to_all(sent, ('core', 'x', 'zl'), split_axis=0, concat_axis=0, ti...  11.1 us
    all_to_all x1, waiting for transfers between devices, body(): lax.all_to_all(sent, ('core', 'x', 'zl'), split_axis=0, concat_axis=0, ti...  3.52 us
  transfers between devices with their start and end apart: 9, of which 3 were waited for; matrix products, arithmetic and copies ran while one was open for 0% of the time, Pallas kernels for 17%

profile of v6, /device:TPU:1, one launch (start us, length us, event | category | flops | bytes accessed | tf_op | source)
XLA Modules:
  0.0 81.4 jit_solution(14443138572526695405)
XLA Ops:
  0.6 0.8 %pad_maximum_fusion = bf16[384,128]{1,0:T(8,128)(2,1)S(1)} fusion(bf16[64,128]{1,0:T(8,128)(2,1)} %bitcast.24, bf16[64,128]{1,0:T(8,128)(2,1)} %bitcast.25, bf16[128,128]{1,0:T(8,128)(2,1)} %bitcast.22, bf16[128,128]{1,0:T(8,128)(2,1)} %bitcast.23), kind=kLoop, calls=%fused_computation | loop fusion | flops 393216 | bytes 196608 | tf_op jit(solution)/shard_map/concatenate | solution.py:203
  1.5 20.0 %all-gather = bf16[1536,128]{1,0:T(8,128)(2,1)S(1)} all-gather(bf16[384,128]{1,0:T(8,128)(2,1)S(1)} %pad_maximum_fusion), channel_id=2, replica_groups=mesh['y'=8,'zh'=4,'x'=4,'zl'=2,'core'=2] {'zh'}, dimensions={0}, use_global_device_ids=true | all-gather | bytes 491520 | tf_op jit(solution)/shard_map/all_gather | solution.py:204
  21.5 5.1 %collective-permute-start = (bf16[4,384,128]{2,1,0:T(8,128)(2,1)S(1)}, bf16[4,384,128]{2,1,0:T(8,128)(2,1)S(1)}, u32[]{:S(2)}, u32[]{:S(2)}) collective-permute-start(bf16[4,384,128]{2,1,0:T(8,128)(2,1)S(1)} %bitcast.12), channel_id=1, source_target_pairs={{0,448},{64,0},{128,64},{192,128},{256,192},{320,256},{384,320},{4... | collective-permute-start | bytes 1179656 | tf_op jit(solution)/shard_map/ppermute | solution.py:35
  26.6 1.9 %collective-permute-start.5 = (bf16[4,384,128]{2,1,0:T(8,128)(2,1)S(1)}, bf16[4,384,128]{2,1,0:T(8,128)(2,1)S(1)}, u32[]{:S(2)}, u32[]{:S(2)}) collective-permute-start(bf16[4,384,128]{2,1,0:T(8,128)(2,1)S(1)} %bitcast.13), channel_id=1, source_target_pairs={{0,64},{64,128},{128,192},{192,256},{256,320},{320,384},{384,448},... | collective-permute-start | bytes 1179656 | tf_op jit(solution)/shard_map/ppermute | solution.py:35
  29.8 0.7 copy-done.1
  30.5 0.2 select_reduce_fusion.pages
  30.7 0.1 pad_add_fusion.scal
  30.8 2.2 %attend_blocks.5 = (f32[1024,128]{1,0:T(8,128)S(1)}, f32[1024,256]{1,0:T(8,128)S(1)}) custom-call(s32[3]{0:T(128)S(1)} %pad_add_fusion.scal, bf16[128,1024]{1,0:T(8,128)(2,1)S(1)} %bitcast.17, bf16[4,384,128]{2,1,0:T(8,128)(2,1)S(1)} %bitcast.14), custom_call_target="tpu_custom_call" | custom-call | flops 4026531840 | bytes 393216 | tf_op jit(solution)/shard_map/attend_blocks/pallas_call | solution.py:124
  33.0 4.6 %collective-permute-start.1 = (bf16[4,384,128]{2,1,0:T(8,128)(2,1)S(1)}, bf16[4,384,128]{2,1,0:T(8,128)(2,1)S(1)}, u32[]{:S(2)}, u32[]{:S(2)}) collective-permute-start(bf16[4,384,128]{2,1,0:T(8,128)(2,1)S(1)} %collective-permute-done.refs_0_.refs_1_), channel_id=1, source_target_pairs={{0,448},{64,0},{128,64},{192,128},{256,192},{320,256},{384,320},{4... | collective-permute-start | bytes 1179656 | tf_op jit(solution)/shard_map/ppermute | solution.py:35
  37.6 1.9 %collective-permute-start.6 = (bf16[4,384,128]{2,1,0:T(8,128)(2,1)S(1)}, bf16[4,384,128]{2,1,0:T(8,128)(2,1)S(1)}, u32[]{:S(2)}, u32[]{:S(2)}) collective-permute-start(bf16[4,384,128]{2,1,0:T(8,128)(2,1)S(1)} %collective-permute-done.5.refs_1_.refs_7_), channel_id=1, source_target_pairs={{0,64},{64,128},{128,192},{192,256},{256,320},{320,384},{384,448},... | collective-permute-start | bytes 1179656 | tf_op jit(solution)/shard_map/ppermute | solution.py:35
  39.5 2.4 %attend_blocks.6 = (f32[1024,128]{1,0:T(8,128)S(1)}, f32[1024,256]{1,0:T(8,128)S(1)}) custom-call(s32[3]{0:T(128)S(1)} %pad_add_fusion.scal, bf16[128,1024]{1,0:T(8,128)(2,1)S(1)} %bitcast.18, bf16[4,384,128]{2,1,0:T(8,128)(2,1)S(1)} %collective-permute-done.refs_0_.refs_1_, ...), custom_call_target="tpu_custom_call", output_to_operand_aliasing={{0}: (4, {}), {1}: (5, {})} | custom-call | flops 8053063680 | bytes 786432 | tf_op jit(solution)/shard_map/attend_blocks/pallas_call | solution.py:124
  41.9 0.6 collective-permute-done.1.refs_0_.refs_2_
  42.5 5.1 %collective-permute-start.2 = (bf16[4,384,128]{2,1,0:T(8,128)(2,1)S(1)}, bf16[4,384,128]{2,1,0:T(8,128)(2,1)S(1)}, u32[]{:S(2)}, u32[]{:S(2)}) collective-permute-start(bf16[4,384,128]{2,1,0:T(8,128)(2,1)S(1)} %collective-permute-done.1.refs_0_.refs_2_), channel_id=1, source_target_pairs={{0,448},{64,0},{128,64},{192,128},{256,192},{320,256},{384,320},{4... | collective-permute-start | bytes 1179656 | tf_op jit(solution)/shard_map/ppermute | solution.py:35
  47.7 1.9 %collective-permute-start.7 = (bf16[4,384,128]{2,1,0:T(8,128)(2,1)S(1)}, bf16[4,384,128]{2,1,0:T(8,128)(2,1)S(1)}, u32[]{:S(2)}, u32[]{:S(2)}) collective-permute-start(bf16[4,384,128]{2,1,0:T(8,128)(2,1)S(1)} %collective-permute-done.6.refs_1_.refs_6_), channel_id=1, source_target_pairs={{0,64},{64,128},{128,192},{192,256},{256,320},{320,384},{384,448},... | collective-permute-start | bytes 1179656 | tf_op jit(solution)/shard_map/ppermute | solution.py:35
  49.6 2.6 %attend_blocks.7 = (f32[1024,128]{1,0:T(8,128)S(1)}, f32[1024,256]{1,0:T(8,128)S(1)}) custom-call(s32[3]{0:T(128)S(1)} %pad_add_fusion.scal, bf16[128,1024]{1,0:T(8,128)(2,1)S(1)} %bitcast.19, bf16[4,384,128]{2,1,0:T(8,128)(2,1)S(1)} %collective-permute-done.1.refs_0_.refs_2_, ...), custom_call_target="tpu_custom_call", output_to_operand_aliasing={{0}: (4, {}), {1}: (5, {})} | custom-call | flops 8053063680 | bytes 786432 | tf_op jit(solution)/shard_map/attend_blocks/pallas_call | solution.py:124
  52.2 0.2 collective-permute-done.2.refs_0_.refs_3_
  52.4 5.5 %collective-permute-start.3 = (bf16[4,256,128]{2,1,0:T(8,128)(2,1)S(1)}, bf16[4,256,128]{2,1,0:T(8,128)(2,1)S(1)}, u32[]{:S(2)}, u32[]{:S(2)}) collective-permute-start(bf16[4,256,128]{2,1,0:T(8,128)(2,1)S(1)} %slice.8), channel_id=1, source_target_pairs={{0,448},{64,0},{128,64},{192,128},{256,192},{320,256},{384,320},{4... | collective-permute-start | bytes 786440 | tf_op jit(solution)/shard_map/ppermute | solution.py:35
  57.9 1.9 %collective-permute-start.4 = (bf16[4,128,128]{2,1,0:T(8,128)(2,1)S(1)}, bf16[4,128,128]{2,1,0:T(8,128)(2,1)S(1)}, u32[]{:S(2)}, u32[]{:S(2)}) collective-permute-start(bf16[4,128,128]{2,1,0:T(8,128)(2,1)S(1)} %slice.9), channel_id=1, source_target_pairs={{0,448},{64,0},{128,64},{192,128},{256,192},{320,256},{384,320},{4... | collective-permute-start | bytes 393224 | tf_op jit(solution)/shard_map/ppermute | solution.py:35
  59.8 2.6 %attend_blocks.8 = (f32[1024,128]{1,0:T(8,128)S(1)}, f32[1024,256]{1,0:T(8,128)S(1)}) custom-call(s32[3]{0:T(128)S(1)} %pad_add_fusion.scal, bf16[128,1024]{1,0:T(8,128)(2,1)S(1)} %bitcast.20, bf16[4,384,128]{2,1,0:T(8,128)(2,1)S(1)} %collective-permute-done.2.refs_0_.refs_3_, ...), custom_call_target="tpu_custom_call", output_to_operand_aliasing={{0}: (4, {}), {1}: (5, {})} | custom-call | flops 8053063680 | bytes 786432 | tf_op jit(solution)/shard_map/attend_blocks/pallas_call | solution.py:124
  62.5 1.4 %pick_pages.1 = bf16[2,8,32,128]{3,2,1,0:T(8,128)(2,1)} custom-call(s32[3]{0:T(128)S(1)} %pad_add_fusion.scal, s32[8]{0:T(128)S(1)} %select_reduce_fusion.pages, bf16[4,384,128]{2,1,0:T(8,128)(2,1)S(1)} %bitcast.15, bf16[4,384,128]{2,1,0:T(8,128)(2,1)S(1)} %collective-permute-done.refs_0_.refs_1_, ...), custom_call_target="tpu_custom_call" | custom-call | tf_op jit(solution)/shard_map/pick_pages/pallas_call | solution.py:168
  63.9 11.1 %all-to-all-start = ((bf16[16,32,128]{2,1,0:T(8,128)(2,1)}), bf16[16,32,128]{2,1,0:T(8,128)(2,1)S(1)}, u32[]{:S(2)}, u32[]{:S(2)}) async-start(bf16[16,32,128]{2,1,0:T(8,128)(2,1)} %bitcast.10), calls=%async_computation | async-start | bytes 262144 | tf_op jit(solution)/shard_map/all_to_all | solution.py:216
  75.0 2.3 %attend_blocks.9 = bf16[128,1024]{1,0:T(8,128)(2,1)} custom-call(s32[3]{0:T(128)S(1)} %pad_add_fusion.scal, bf16[128,1024]{1,0:T(8,128)(2,1)S(1)} %bitcast.21, bf16[4,256,128]{2,1,0:T(8,128)(2,1)S(1)} %collective-permute-done.3.refs_0_.refs_4_, bf16[4,128,128]{2,1,0:T(8,128)(2,1)S(1)} %collective-permute-done.4.refs_1_, ...), custom_call_target="tpu_custom_call" | custom-call | flops 4026531840 | bytes 393216 | tf_op jit(solution)/shard_map/attend_blocks/pallas_call | solution.py:124
  77.3 3.5 %all-to-all-done = bf16[16,32,128]{2,1,0:T(8,128)(2,1)S(1)} async-done(((bf16[16,32,128]{2,1,0:T(8,128)(2,1)}), bf16[16,32,128]{2,1,0:T(8,128)(2,1)S(1)}, u32[]{:S(2)}, u32[]{:S(2)}) %all-to-all-start) | async-done | bytes 131104 | tf_op jit(solution)/shard_map/all_to_all | solution.py:216
  80.8 0.6 assemble_pages.1
  (12 shorter events, 0.1 us)
Async XLA Ops:
  1.4 29.3 %copy-start = (bf16[1,128,1024]{2,1,0:T(8,128)(2,1)S(1)}, bf16[1,128,1024]{2,1,0:T(8,128)(2,1)}, u32[]{:S(2)}) copy-start(bf16[1,128,1024]{2,1,0:T(8,128)(2,1)} %param.8) | copy-start | bytes 786436
  21.5 11.5 %collective-permute-start = (bf16[4,384,128]{2,1,0:T(8,128)(2,1)S(1)}, bf16[4,384,128]{2,1,0:T(8,128)(2,1)S(1)}, u32[]{:S(2)}, u32[]{:S(2)}) collective-permute-start(bf16[4,384,128]{2,1,0:T(8,128)(2,1)S(1)} %bitcast.12), channel_id=1, source_target_pairs={{0,448},{64,0},{128,64},{192,128},{256,192},{320,256},{384,320},{4... | collective-permute-start | bytes 1179656 | tf_op jit(solution)/shard_map/ppermute | solution.py:35
  26.6 11.0 %collective-permute-start.5 = (bf16[4,384,128]{2,1,0:T(8,128)(2,1)S(1)}, bf16[4,384,128]{2,1,0:T(8,128)(2,1)S(1)}, u32[]{:S(2)}, u32[]{:S(2)}) collective-permute-start(bf16[4,384,128]{2,1,0:T(8,128)(2,1)S(1)} %bitcast.13), channel_id=1, source_target_pairs={{0,64},{64,128},{128,192},{192,256},{256,320},{320,384},{384,448},... | collective-permute-start | bytes 1179656 | tf_op jit(solution)/shard_map/ppermute | solution.py:35
  29.8 0.7 copy-start.1
  33.0 9.5 %collective-permute-start.1 = (bf16[4,384,128]{2,1,0:T(8,128)(2,1)S(1)}, bf16[4,384,128]{2,1,0:T(8,128)(2,1)S(1)}, u32[]{:S(2)}, u32[]{:S(2)}) collective-permute-start(bf16[4,384,128]{2,1,0:T(8,128)(2,1)S(1)} %collective-permute-done.refs_0_.refs_1_), channel_id=1, source_target_pairs={{0,448},{64,0},{128,64},{192,128},{256,192},{320,256},{384,320},{4... | collective-permute-start | bytes 1179656 | tf_op jit(solution)/shard_map/ppermute | solution.py:35
  37.6 10.1 %collective-permute-start.6 = (bf16[4,384,128]{2,1,0:T(8,128)(2,1)S(1)}, bf16[4,384,128]{2,1,0:T(8,128)(2,1)S(1)}, u32[]{:S(2)}, u32[]{:S(2)}) collective-permute-start(bf16[4,384,128]{2,1,0:T(8,128)(2,1)S(1)} %collective-permute-done.5.refs_1_.refs_7_), channel_id=1, source_target_pairs={{0,64},{64,128},{128,192},{192,256},{256,320},{320,384},{384,448},... | collective-permute-start | bytes 1179656 | tf_op jit(solution)/shard_map/ppermute | solution.py:35
  42.5 9.9 %collective-permute-start.2 = (bf16[4,384,128]{2,1,0:T(8,128)(2,1)S(1)}, bf16[4,384,128]{2,1,0:T(8,128)(2,1)S(1)}, u32[]{:S(2)}, u32[]{:S(2)}) collective-permute-start(bf16[4,384,128]{2,1,0:T(8,128)(2,1)S(1)} %collective-permute-done.1.refs_0_.refs_2_), channel_id=1, source_target_pairs={{0,448},{64,0},{128,64},{192,128},{256,192},{320,256},{384,320},{4... | collective-permute-start | bytes 1179656 | tf_op jit(solution)/shard_map/ppermute | solution.py:35
  47.7 12.2 %collective-permute-start.7 = (bf16[4,384,128]{2,1,0:T(8,128)(2,1)S(1)}, bf16[4,384,128]{2,1,0:T(8,128)(2,1)S(1)}, u32[]{:S(2)}, u32[]{:S(2)}) collective-permute-start(bf16[4,384,128]{2,1,0:T(8,128)(2,1)S(1)} %collective-permute-done.6.refs_1_.refs_6_), channel_id=1, source_target_pairs={{0,64},{64,128},{128,192},{192,256},{256,320},{320,384},{384,448},... | collective-permute-start | bytes 1179656 | tf_op jit(solution)/shard_map/ppermute | solution.py:35
  52.4 10.1 %collective-permute-start.3 = (bf16[4,256,128]{2,1,0:T(8,128)(2,1)S(1)}, bf16[4,256,128]{2,1,0:T(8,128)(2,1)S(1)}, u32[]{:S(2)}, u32[]{:S(2)}) collective-permute-start(bf16[4,256,128]{2,1,0:T(8,128)(2,1)S(1)} %slice.8), channel_id=1, source_target_pairs={{0,448},{64,0},{128,64},{192,128},{256,192},{320,256},{384,320},{4... | collective-permute-start | bytes 786440 | tf_op jit(solution)/shard_map/ppermute | solution.py:35
  57.9 17.1 %collective-permute-start.4 = (bf16[4,128,128]{2,1,0:T(8,128)(2,1)S(1)}, bf16[4,128,128]{2,1,0:T(8,128)(2,1)S(1)}, u32[]{:S(2)}, u32[]{:S(2)}) collective-permute-start(bf16[4,128,128]{2,1,0:T(8,128)(2,1)S(1)} %slice.9), channel_id=1, source_target_pairs={{0,448},{64,0},{128,64},{192,128},{256,192},{320,256},{384,320},{4... | collective-permute-start | bytes 393224 | tf_op jit(solution)/shard_map/ppermute | solution.py:35
  63.9 16.9 %all-to-all-start = ((bf16[16,32,128]{2,1,0:T(8,128)(2,1)}), bf16[16,32,128]{2,1,0:T(8,128)(2,1)S(1)}, u32[]{:S(2)}, u32[]{:S(2)}) async-start(bf16[16,32,128]{2,1,0:T(8,128)(2,1)} %bitcast.10), calls=%async_computation | async-start | bytes 262144 | tf_op jit(solution)/shard_map/all_to_all | solution.py:216
